TPU v7x, 256 devices: a whole 4x4x8 slice. The times are simulated.
256 devices in a mesh: tgt: 32 (over z_lo, y, core), src: 8 (over x, z_hi).
Axes of the slice: x: 4, y: 4, z: 8 (z_hi: 2, z_lo: 4; z = z_hi * 4 + z_lo), core: 2. Of those that a mesh axis runs over, the one named last changes fastest.
Arguments:
- positions: float32 [1024, 3, 642], P(('tgt', 'src')), may hold values from -1.1 to 358.4, as said below
- weights: float32 [1024, 642], P(('tgt', 'src')), may hold values from 0.0062305294 to 0.062305298
- density: float32 [1024, 3, 642], P(('tgt', 'src')), may hold values from -6 to 6
- near_source: int32 [1024, 8], P(('tgt', 'src')), may hold values from -1 to 1023, as said below
- couplings: bfloat16 [1024, 1024, 16, 16], P('tgt', 'src'), may hold values from -0.046875 to 0.046875
- source_basis: bfloat16 [1024, 16, 3, 642], P(('tgt', 'src')), may hold values from -0.125 to 0.125
- target_basis: bfloat16 [1024, 16, 3, 642], P(('tgt', 'src')), may hold values from -1.5 to 1.5
Outputs:
- velocity: float32 [1024, 3, 642], P(('tgt', 'src'))
Inputs may be any that keep to these rules, and one draw needn't show every extreme that they name: `positions`: nodes of two different bodies are at least 0.1 apart. `near_source`: row i holds between 1 and 8 distinct bodies other than i, all in the same block of 32 consecutive bodies as i or in the block just before or after it; the used slots come first and the rest hold -1. Some rows use all 8 slots.
All inputs are finite; a program needn't handle non-finite values.
Results may differ from a plain program's by a relative error of at most 0.0033.
Values may be sent and summed in bfloat16 or wider, within the bound.
A program may use at most 64 MiB of HBM per device.

v0:
```python
import jax
import jax.numpy as jnp
from jax import lax
from jax.sharding import PartitionSpec as P


def with_halo(block, sides, width):
    for axis, dim in sides:
        count = lax.axis_size(axis)
        forward = [(i, i + 1) for i in range(count - 1)]
        backward = [(target, source) for source, target in forward]
        low = lax.ppermute(
            lax.slice_in_dim(block, block.shape[dim] - width, None, axis=dim), axis, forward
        )
        high = lax.ppermute(lax.slice_in_dim(block, 0, width, axis=dim), axis, backward)
        block = jnp.concatenate([low, block, high], axis=dim)
    return block


def stokeslet(target, source):
    weighted = source[3:6] * source[6:7]
    delta_x = target[0][:, None] - source[0][None, :]
    delta_y = target[1][:, None] - source[1][None, :]
    delta_z = target[2][:, None] - source[2][None, :]
    squared = delta_x * delta_x + delta_y * delta_y + delta_z * delta_z
    inverse = 1.0 / jnp.sqrt(squared)
    cubed = inverse * inverse * inverse
    along = (
        delta_x * weighted[0][None, :]
        + delta_y * weighted[1][None, :]
        + delta_z * weighted[2][None, :]
    )
    pull = along * cubed
    first = jnp.sum(weighted[0][None, :] * inverse + delta_x * pull, axis=1)
    second = jnp.sum(weighted[1][None, :] * inverse + delta_y * pull, axis=1)
    third = jnp.sum(weighted[2][None, :] * inverse + delta_z * pull, axis=1)
    return jnp.stack([first, second, third], 0)


def group_length():
    for length_try in (4, 3, 2, 1):
        return length_try
    return 1


def near_field(near_pack, sources, target_base, base):
    rows, per_row = sources.shape
    group = group_length()
    blocks = rows // group
    nodes = near_pack.shape[2]
    active = sources >= 0
    offsets = jnp.where(active, sources - base, 0)

    def advance(turn, total):
        column = (turn // blocks).astype(jnp.int32)
        first = (turn % blocks * group).astype(jnp.int32)
        keeping = lax.dynamic_slice(active, (first, column), (group, 1))[:, 0]
        picked = lax.dynamic_slice(offsets, (first, column), (group, 1))[:, 0]

        def evaluate(current):
            targets = lax.dynamic_slice_in_dim(near_pack, target_base + first, group, 0)[:, 0:3]
            sources_now = near_pack[picked]
            values = jax.vmap(stokeslet)(targets, sources_now)
            values = jnp.where(keeping[:, None, None], values, jnp.float32(0.0))
            earlier = lax.dynamic_slice_in_dim(current, first, group, 0)
            return lax.dynamic_update_slice_in_dim(current, earlier + values, first, 0)

        def unchanged(current):
            return current

        return lax.cond(jnp.any(keeping), evaluate, unchanged, total)

    start = jnp.zeros((rows, 3, nodes), jnp.float32)
    return lax.fori_loop(0, per_row * blocks, advance, start)


def local(positions, weights, density, near_source, couplings, source_basis, target_basis):
    owned = positions.shape[0]
    slots = near_source.shape[1]
    src_count = lax.axis_size("src")
    tgt_count = lax.axis_size("tgt")
    row_len = owned * src_count
    block_len = owned * tgt_count
    src_place = lax.axis_index("src")
    tgt_place = lax.axis_index("tgt")
    row_first = tgt_place * row_len
    coef = jnp.einsum(
        "brcp,bcp->br", source_basis.astype(jnp.float32), density, precision=lax.Precision.HIGHEST
    )
    every_coef = lax.all_gather(coef.astype(jnp.bfloat16), ("tgt", "src"), axis=0, tiled=True)
    block_coef = lax.dynamic_slice_in_dim(every_coef, src_place * block_len, block_len, 0)
    row_lists = lax.all_gather(near_source, "src", axis=0, tiled=True)
    source_ids = src_place * block_len + jnp.arange(block_len, dtype=jnp.int32)
    target_ids = row_first + jnp.arange(row_len, dtype=jnp.int32)
    listed = jnp.any(row_lists[:, :, None] == source_ids[None, None, :], axis=1)
    itself = target_ids[:, None] == source_ids[None, :]
    keep = jnp.logical_not(jnp.logical_or(listed, itself))
    masked = jnp.where(keep[:, :, None], block_coef[None, :, :], jnp.zeros((), jnp.bfloat16))
    far_part = jnp.einsum("ijrs,ijs->ir", couplings, masked, preferred_element_type=jnp.float32)
    packed = jnp.concatenate([positions, density, weights[:, None, :]], axis=1)
    row_pack = lax.all_gather(packed, "src", axis=0, tiled=True)
    near_pack = with_halo(row_pack, (("tgt", 0),), row_len)
    base = row_first - row_len
    per_device = slots // src_count
    slot_ids = src_place + src_count * jnp.arange(per_device, dtype=jnp.int32)
    picked = jnp.take(row_lists, slot_ids, axis=1)
    near_part = near_field(near_pack, picked, jnp.int32(row_len), base)
    near_own, coupled = (
        lax.psum_scatter(near_part, "src", scatter_dimension=0, tiled=True),
        lax.psum_scatter(far_part, "src", scatter_dimension=0, tiled=True),
    )
    far_velocity = jnp.einsum(
        "brcp,br->bcp",
        target_basis,
        coupled.astype(jnp.bfloat16),
        preferred_element_type=jnp.float32,
    )
    return far_velocity + near_own


def solution(mesh):
    placed = (
        P(("tgt", "src"), None, None),
        P(("tgt", "src"), None),
        P(("tgt", "src"), None, None),
        P(("tgt", "src"), None),
        P("tgt", "src", None, None),
        P(("tgt", "src"), None, None, None),
        P(("tgt", "src"), None, None, None),
    )
    return jax.shard_map(
        local, mesh=mesh, in_specs=placed, out_specs=P(("tgt", "src"), None, None), check_vma=False
    )
```

profile of v0, /device:TPU:64, one launch (start us, length us, event | category | flops | bytes accessed | tf_op | source)
XLA Modules:
  0.0 1290.4 jit_solution(18177347198999278909)
XLA Ops:
  9.1 55.8 %all_gather.11 = f32[32,7,642]{2,1,0:T(8,128)S(1)} all-gather(f32[4,7,642]{2,1,0:T(8,128)S(1)} %pad_maximum_fusion.1), channel_id=1, replica_groups=mesh['tgt'=32,'src'=8] {'src'}, dimensions={0}, use_global_device_ids=true | all-gather | bytes 647136 | tf_op jit(solution)/shard_map/all_gather | solution.py:101
  65.9 1.9 collective-permute-start
  67.9 5.8 collective-permute-start.1
  73.6 40.2 %all-gather = s32[8,4,8]{2,1,0:T(4,128)S(1)} all-gather(s32[1,4,8]{2,1,0:T(4,128)S(1)} %bitcast.70), channel_id=1, replica_groups=mesh['tgt'=32,'src'=8] {'src'}, dimensions={0}, use_global_device_ids=true | all-gather | bytes 1152 | tf_op jit(solution)/shard_map/all_gather | solution.py:92
  114.2 735.6 %all-gather.1 = bf16[256,4,16]{2,1,0:T(4,128)(2,1)S(1)} all-gather(bf16[1,4,16]{2,1,0:T(4,128)(2,1)S(1)} %convert_bitcast_fusion), channel_id=1, replica_groups=mesh['tgt'=32,'src'=8] {'tgt','src'}, dimensions={0}, use_global_device_ids=true | all-gather | bytes 32896 | tf_op jit(solution)/shard_map/all_gather | solution.py:90
  850.0 1.5 select_bitcast_fusion
  851.6 1.7 copy.61
  855.6 52.5 %all-reduce = bf16[32,16]{1,0:T(8,128)(2,1)S(1)} all-reduce(f32[32,16]{1,0:T(8,128)S(1)} %bitcast.69), channel_id=2, replica_groups=mesh['tgt'=32,'src'=8] {'src'}, use_global_device_ids=true, to_apply=%region_1.2.clone | all-reduce | flops 512 | bytes 3072
  908.1 1.5 copy.57
  909.6 1.5 copy.58
  911.1 1.7 pad_maximum_fusion
  913.5 263.0 %while.19 = (s32[]{:T(128)}, f32[32,3,642]{2,0,1:T(8,128)}, pred[32,1]{0,1:T(4,128)(4,1)S(1)}, f32[96,7,642]{2,1,0:T(8,128)}, s32[32,1]{0,1:T(1,128)S(1)}, /*ind...) while((s32[]{:T(128)}, f32[32,3,642]{2,0,1:T(8,128)}, ...), condition=%wide.region_9.10_spmd, body=%wide.region_2.9_spmd.sunk | while | flops 46194240 | bytes 970135 | solution.py:74
  914.7 31.6 %conditional.2 = (f32[32,3,642]{2,0,1:T(8,128)}) conditional(s32[]{:T(128)} %convert_element_type.24, f32[32,3,642]{2,0,1:T(8,128)} %get-tuple-element.275, (s32[]{:T(128)}, f32[32,3,642]{2,0,1:T(8,128)}, pred[4,1]{0,1:T(4,128)(4,1)S(1)}, f32[96,7,642]{2,1,0:T(8,128)}, s32[32,1]{0,1:T(1,128)S(1)}, /*index=5*/s32[]{:T(128)}) %tuple.72), branch_computations={%region_4.4_spmd, %region_5.8_spmd} | conditional | flops 46194224 | bytes 969856 | solution.py:71
  916.5 2.2 gather_fusion
  918.9 22.5 %fusion.7 = (f32[4,642]{0,1:T(8,128)}, f32[4,642]{0,1:T(8,128)S(1)}, f32[4,642]{0,1:T(8,128)}) fusion(f32[4,642]{1,0:T(4,128)S(1)} %bitcast.64, f32[4,642]{1,0:T(4,128)S(1)} %get-tuple-element.227, f32[4,642]{0,1:T(8,128)S(1)} %bitcast.55, f32[4,642]{1,0:T(4,128)S(1)} %get-tuple-element.225, f32[4,642]{0,1:T(8,128)S(1)} %bitcast.57, ...), kind=kLoop, calls=%fused_computation.18 | loop fusion | flops 46154664 | bytes 123264 | tf_op jit(solution)/shard_map/while/body/eval_jaxpr/cond/branch_1_fun/vmap()/reduce_sum | solution.py:34
  942.5 1.1 copy.50
  944.8 1.6 dynamic_update_slice.3
  947.6 31.6 %conditional.2 = (f32[32,3,642]{2,0,1:T(8,128)}) conditional(s32[]{:T(128)} %convert_element_type.24, f32[32,3,642]{2,0,1:T(8,128)} %get-tuple-element.275, (s32[]{:T(128)}, f32[32,3,642]{2,0,1:T(8,128)}, pred[4,1]{0,1:T(4,128)(4,1)S(1)}, f32[96,7,642]{2,1,0:T(8,128)}, s32[32,1]{0,1:T(1,128)S(1)}, /*index=5*/s32[]{:T(128)}) %tuple.72), branch_computations={%region_4.4_spmd, %region_5.8_spmd} | conditional | flops 46194224 | bytes 969856 | solution.py:71
  949.4 2.2 gather_fusion
  951.8 22.5 %fusion.7 = (f32[4,642]{0,1:T(8,128)}, f32[4,642]{0,1:T(8,128)S(1)}, f32[4,642]{0,1:T(8,128)}) fusion(f32[4,642]{1,0:T(4,128)S(1)} %bitcast.64, f32[4,642]{1,0:T(4,128)S(1)} %get-tuple-element.227, f32[4,642]{0,1:T(8,128)S(1)} %bitcast.55, f32[4,642]{1,0:T(4,128)S(1)} %get-tuple-element.225, f32[4,642]{0,1:T(8,128)S(1)} %bitcast.57, ...), kind=kLoop, calls=%fused_computation.18 | loop fusion | flops 46154664 | bytes 123264 | tf_op jit(solution)/shard_map/while/body/eval_jaxpr/cond/branch_1_fun/vmap()/reduce_sum | solution.py:34
  975.4 1.1 copy.50
  977.7 1.6 dynamic_update_slice.3
  980.5 31.6 %conditional.2 = (f32[32,3,642]{2,0,1:T(8,128)}) conditional(s32[]{:T(128)} %convert_element_type.24, f32[32,3,642]{2,0,1:T(8,128)} %get-tuple-element.275, (s32[]{:T(128)}, f32[32,3,642]{2,0,1:T(8,128)}, pred[4,1]{0,1:T(4,128)(4,1)S(1)}, f32[96,7,642]{2,1,0:T(8,128)}, s32[32,1]{0,1:T(1,128)S(1)}, /*index=5*/s32[]{:T(128)}) %tuple.72), branch_computations={%region_4.4_spmd, %region_5.8_spmd} | conditional | flops 46194224 | bytes 969856 | solution.py:71
  982.3 2.2 gather_fusion
  984.7 22.5 %fusion.7 = (f32[4,642]{0,1:T(8,128)}, f32[4,642]{0,1:T(8,128)S(1)}, f32[4,642]{0,1:T(8,128)}) fusion(f32[4,642]{1,0:T(4,128)S(1)} %bitcast.64, f32[4,642]{1,0:T(4,128)S(1)} %get-tuple-element.227, f32[4,642]{0,1:T(8,128)S(1)} %bitcast.55, f32[4,642]{1,0:T(4,128)S(1)} %get-tuple-element.225, f32[4,642]{0,1:T(8,128)S(1)} %bitcast.57, ...), kind=kLoop, calls=%fused_computation.18 | loop fusion | flops 46154664 | bytes 123264 | tf_op jit(solution)/shard_map/while/body/eval_jaxpr/cond/branch_1_fun/vmap()/reduce_sum | solution.py:34
  1010.5 1.6 dynamic_update_slice.3
  1013.4 31.6 %conditional.2 = (f32[32,3,642]{2,0,1:T(8,128)}) conditional(s32[]{:T(128)} %convert_element_type.24, f32[32,3,642]{2,0,1:T(8,128)} %get-tuple-element.275, (s32[]{:T(128)}, f32[32,3,642]{2,0,1:T(8,128)}, pred[4,1]{0,1:T(4,128)(4,1)S(1)}, f32[96,7,642]{2,1,0:T(8,128)}, s32[32,1]{0,1:T(1,128)S(1)}, /*index=5*/s32[]{:T(128)}) %tuple.72), branch_computations={%region_4.4_spmd, %region_5.8_spmd} | conditional | flops 46194224 | bytes 969856 | solution.py:71
  1015.2 2.2 gather_fusion
  1017.6 22.5 %fusion.7 = (f32[4,642]{0,1:T(8,128)}, f32[4,642]{0,1:T(8,128)S(1)}, f32[4,642]{0,1:T(8,128)}) fusion(f32[4,642]{1,0:T(4,128)S(1)} %bitcast.64, f32[4,642]{1,0:T(4,128)S(1)} %get-tuple-element.227, f32[4,642]{0,1:T(8,128)S(1)} %bitcast.55, f32[4,642]{1,0:T(4,128)S(1)} %get-tuple-element.225, f32[4,642]{0,1:T(8,128)S(1)} %bitcast.57, ...), kind=kLoop, calls=%fused_computation.18 | loop fusion | flops 46154664 | bytes 123264 | tf_op jit(solution)/shard_map/while/body/eval_jaxpr/cond/branch_1_fun/vmap()/reduce_sum | solution.py:34
  1043.4 1.6 dynamic_update_slice.3
  1046.3 31.6 %conditional.2 = (f32[32,3,642]{2,0,1:T(8,128)}) conditional(s32[]{:T(128)} %convert_element_type.24, f32[32,3,642]{2,0,1:T(8,128)} %get-tuple-element.275, (s32[]{:T(128)}, f32[32,3,642]{2,0,1:T(8,128)}, pred[4,1]{0,1:T(4,128)(4,1)S(1)}, f32[96,7,642]{2,1,0:T(8,128)}, s32[32,1]{0,1:T(1,128)S(1)}, /*index=5*/s32[]{:T(128)}) %tuple.72), branch_computations={%region_4.4_spmd, %region_5.8_spmd} | conditional | flops 46194224 | bytes 969856 | solution.py:71
  1048.1 2.2 gather_fusion
  1050.5 22.5 %fusion.7 = (f32[4,642]{0,1:T(8,128)}, f32[4,642]{0,1:T(8,128)S(1)}, f32[4,642]{0,1:T(8,128)}) fusion(f32[4,642]{1,0:T(4,128)S(1)} %bitcast.64, f32[4,642]{1,0:T(4,128)S(1)} %get-tuple-element.227, f32[4,642]{0,1:T(8,128)S(1)} %bitcast.55, f32[4,642]{1,0:T(4,128)S(1)} %get-tuple-element.225, f32[4,642]{0,1:T(8,128)S(1)} %bitcast.57, ...), kind=kLoop, calls=%fused_computation.18 | loop fusion | flops 46154664 | bytes 123264 | tf_op jit(solution)/shard_map/while/body/eval_jaxpr/cond/branch_1_fun/vmap()/reduce_sum | solution.py:34
  1076.3 1.6 dynamic_update_slice.3
  1079.2 31.6 %conditional.2 = (f32[32,3,642]{2,0,1:T(8,128)}) conditional(s32[]{:T(128)} %convert_element_type.24, f32[32,3,642]{2,0,1:T(8,128)} %get-tuple-element.275, (s32[]{:T(128)}, f32[32,3,642]{2,0,1:T(8,128)}, pred[4,1]{0,1:T(4,128)(4,1)S(1)}, f32[96,7,642]{2,1,0:T(8,128)}, s32[32,1]{0,1:T(1,128)S(1)}, /*index=5*/s32[]{:T(128)}) %tuple.72), branch_computations={%region_4.4_spmd, %region_5.8_spmd} | conditional | flops 46194224 | bytes 969856 | solution.py:71
  1080.9 2.2 gather_fusion
  1083.3 22.5 %fusion.7 = (f32[4,642]{0,1:T(8,128)}, f32[4,642]{0,1:T(8,128)S(1)}, f32[4,642]{0,1:T(8,128)}) fusion(f32[4,642]{1,0:T(4,128)S(1)} %bitcast.64, f32[4,642]{1,0:T(4,128)S(1)} %get-tuple-element.227, f32[4,642]{0,1:T(8,128)S(1)} %bitcast.55, f32[4,642]{1,0:T(4,128)S(1)} %get-tuple-element.225, f32[4,642]{0,1:T(8,128)S(1)} %bitcast.57, ...), kind=kLoop, calls=%fused_computation.18 | loop fusion | flops 46154664 | bytes 123264 | tf_op jit(solution)/shard_map/while/body/eval_jaxpr/cond/branch_1_fun/vmap()/reduce_sum | solution.py:34
  1109.2 1.6 dynamic_update_slice.3
  1112.1 31.6 %conditional.2 = (f32[32,3,642]{2,0,1:T(8,128)}) conditional(s32[]{:T(128)} %convert_element_type.24, f32[32,3,642]{2,0,1:T(8,128)} %get-tuple-element.275, (s32[]{:T(128)}, f32[32,3,642]{2,0,1:T(8,128)}, pred[4,1]{0,1:T(4,128)(4,1)S(1)}, f32[96,7,642]{2,1,0:T(8,128)}, s32[32,1]{0,1:T(1,128)S(1)}, /*index=5*/s32[]{:T(128)}) %tuple.72), branch_computations={%region_4.4_spmd, %region_5.8_spmd} | conditional | flops 46194224 | bytes 969856 | solution.py:71
  1113.8 2.2 gather_fusion
  1116.2 22.5 %fusion.7 = (f32[4,642]{0,1:T(8,128)}, f32[4,642]{0,1:T(8,128)S(1)}, f32[4,642]{0,1:T(8,128)}) fusion(f32[4,642]{1,0:T(4,128)S(1)} %bitcast.64, f32[4,642]{1,0:T(4,128)S(1)} %get-tuple-element.227, f32[4,642]{0,1:T(8,128)S(1)} %bitcast.55, f32[4,642]{1,0:T(4,128)S(1)} %get-tuple-element.225, f32[4,642]{0,1:T(8,128)S(1)} %bitcast.57, ...), kind=kLoop, calls=%fused_computation.18 | loop fusion | flops 46154664 | bytes 123264 | tf_op jit(solution)/shard_map/while/body/eval_jaxpr/cond/branch_1_fun/vmap()/reduce_sum | solution.py:34
  1142.1 1.6 dynamic_update_slice.3
  1144.9 31.6 %conditional.2 = (f32[32,3,642]{2,0,1:T(8,128)}) conditional(s32[]{:T(128)} %convert_element_type.24, f32[32,3,642]{2,0,1:T(8,128)} %get-tuple-element.275, (s32[]{:T(128)}, f32[32,3,642]{2,0,1:T(8,128)}, pred[4,1]{0,1:T(4,128)(4,1)S(1)}, f32[96,7,642]{2,1,0:T(8,128)}, s32[32,1]{0,1:T(1,128)S(1)}, /*index=5*/s32[]{:T(128)}) %tuple.72), branch_computations={%region_4.4_spmd, %region_5.8_spmd} | conditional | flops 46194224 | bytes 969856 | solution.py:71
  1146.6 2.2 gather_fusion
  1149.0 22.5 %fusion.7 = (f32[4,642]{0,1:T(8,128)}, f32[4,642]{0,1:T(8,128)S(1)}, f32[4,642]{0,1:T(8,128)}) fusion(f32[4,642]{1,0:T(4,128)S(1)} %bitcast.64, f32[4,642]{1,0:T(4,128)S(1)} %get-tuple-element.227, f32[4,642]{0,1:T(8,128)S(1)} %bitcast.55, f32[4,642]{1,0:T(4,128)S(1)} %get-tuple-element.225, f32[4,642]{0,1:T(8,128)S(1)} %bitcast.57, ...), kind=kLoop, calls=%fused_computation.18 | loop fusion | flops 46154664 | bytes 123264 | tf_op jit(solution)/shard_map/while/body/eval_jaxpr/cond/branch_1_fun/vmap()/reduce_sum | solution.py:34
  1174.9 1.6 dynamic_update_slice.3
  1177.6 104.4 %all-reduce.4.cloned.1.call-done = f32[32,3,642]{2,0,1:T(8,128)} async-done(((f32[32,3,642]{2,0,1:T(8,128)}), f32[32,3,642]{2,0,1:T(8,128)}) %all-reduce.4.cloned.1.call-update) | async-done | bytes 246544
  1282.1 1.5 dynamic-slice_add_fusion
  (185 shorter events, 52.9 us)
Async XLA Ops:
  6.5 846.8 %copy-start = (bf16[32,128,16,16]{1,3,2,0:T(8,128)(2,1)S(1)}, bf16[32,128,16,16]{1,3,2,0:T(8,128)(2,1)}, u32[]{:S(2)}) copy-start(bf16[32,128,16,16]{1,3,2,0:T(8,128)(2,1)} %param.15) | copy-start | bytes 6291460
  6.5 107.3 %copy-start.1 = (f32[4,3,642]{2,0,1:T(4,128)S(1)}, f32[4,3,642]{2,0,1:T(4,128)}, u32[]{:S(2)}) copy-start(f32[4,3,642]{2,0,1:T(4,128)} %param.13) | copy-start | bytes 92452
  6.5 67.1 %copy-start.2 = (s32[4,8]{1,0:T(4,128)S(1)}, s32[4,8]{1,0:T(4,128)}, u32[]{:S(2)}) copy-start(s32[4,8]{1,0:T(4,128)} %param.14) | copy-start | bytes 388
  6.5 107.3 %copy-start.3 = (bf16[4,16,3,642]{3,1,2,0:T(8,128)(2,1)S(1)}, bf16[4,16,3,642]{3,1,2,0:T(8,128)(2,1)}, u32[]{:S(2)}) copy-start(bf16[4,16,3,642]{3,1,2,0:T(8,128)(2,1)} %param.16) | copy-start | bytes 739588
  6.5 1275.5 %all-reduce.4.cloned.1.call-start = ((), (), s32[]{:S(2)}) async-start(), calls=%async_computation | async-start | bytes 589824
  65.9 842.1 %collective-permute-start = (f32[32,7,642]{2,0,1:T(8,128)}, f32[32,7,642]{2,0,1:T(8,128)}, u32[]{:S(2)}, u32[]{:S(2)}) collective-permute-start(f32[32,7,642]{2,0,1:T(8,128)} %copy.55), channel_id=1, source_target_pairs={{0,8},{8,16},{16,24},{24,32},{32,40},{40,48},{48,56},{56,64},{64,7... | collective-permute-start | bytes 1725704 | tf_op jit(solution)/shard_map/ppermute | solution.py:12
  67.9 841.7 %collective-permute-start.1 = (f32[32,7,642]{2,0,1:T(8,128)}, f32[32,7,642]{2,0,1:T(8,128)}, u32[]{:S(2)}, u32[]{:S(2)}) collective-permute-start(f32[32,7,642]{2,0,1:T(8,128)} %copy.55), channel_id=1, source_target_pairs={{8,0},{16,8},{24,16},{32,24},{40,32},{48,40},{56,48},{64,56},{72,6... | collective-permute-start | bytes 1725704 | tf_op jit(solution)/shard_map/ppermute | solution.py:15
  851.6 2.8 copy-start.4
Sparse Core Ops, SparseCore 0:
  1176.6 105.4 all-reduce.3
where the time goes:
time: 1290 us
  blocking collectives  884 us (69%)
  other arithmetic  199 us (15%)
  waiting for transfers between devices  104 us (8%)
  local copies, waits for them, and re-layouts  73.2 us (6%)
  between operations  14.1 us (1%)
    all_gather x1, blocking collectives, local(): lax.all_gather(coef.astype(jnp.bfloat16), ('tgt', 'src'), axis=0, tiled=T...  736 us
    reduce_sum x8, other arithmetic, stokeslet(): first = jnp.sum(weighted[0][None, :] * inverse + delta_x * pull, axis=1)  180 us
    unnamed x2, waiting for transfers between devices  104 us
    all_gather x1, blocking collectives, local(): row_pack = lax.all_gather(packed, 'src', axis=0, tiled=True)  55.8 us
    unnamed x1, blocking collectives  52.5 us
    all_gather x1, blocking collectives, local(): row_lists = lax.all_gather(near_source, 'src', axis=0, tiled=True)  40.2 us
  transfers between devices with their start and end apart: 3, of which 1 were waited for; matrix products, arithmetic and copies ran while one was open for 1% of the time, Pallas kernels for 0%

commit v1 on v0

v1 whole, which is shorter than its diff:
```python
import functools
import jax
import jax.numpy as jnp
from jax import lax
from jax.experimental import pallas as pl
from jax.experimental.pallas import tpu as pltpu
from jax.sharding import PartitionSpec as P

F32 = jnp.float32
BF16 = jnp.bfloat16
LANES = 768
ROWS = 656
MAIN = 640
COMPS = 6
FAR_AWAY = 1000.0
LEAST_GAP = 0.1
MOST_RATIO = 70.0
MESH = pl.DeviceIdType.MESH


def remote(source, target, send, recv, device):
    return pltpu.make_async_remote_copy(
        src_ref=source,
        dst_ref=target,
        send_sem=send,
        recv_sem=recv,
        device_id=device,
        device_id_type=MESH,
    )


def exchange_kernel(
    nodes,
    positions,
    weights,
    density,
    near,
    couplings,
    basis,
    geometry,
    coupled,
    held,
    coef_mine,
    coef_relay,
    coef_sum,
    coef_parts,
    lists,
    mask,
    folded,
    far_mine,
    far_parts,
    held_sem,
    list_send,
    list_recv,
    first_send,
    first_recv,
    second_send,
    second_recv,
    far_send,
    far_recv,
    row_send,
    row_recv,
    halo_send,
    halo_recv,
):
    t = lax.axis_index("tgt")
    s = lax.axis_index("src")
    t_count = lax.axis_size("tgt")
    x = s // 2
    z = s % 2
    group = t // 8
    place = t % 8
    quarter = t // 4
    own = positions.shape[1]
    loops_back = jnp.logical_and(quarter == s, place == s)

    load = pltpu.make_async_copy(couplings, held, held_sem)
    load.start()

    barrier = pltpu.get_barrier_semaphore()

    def greet(device):
        pl.semaphore_signal(barrier, inc=1, device_id=device, device_id_type=MESH)

    for step in range(1, 8):
        greet((t, (s + step) % 8))
        greet((group * 8 + (place + step) % 8, s))
    for part in range(4):

        @pl.when(jnp.logical_not(jnp.logical_and(loops_back, part == t % 4)))
        def _():
            greet((4 * s + part, place))

    @pl.when(t > 0)
    def _():
        greet((t - 1, s))

    @pl.when(t < t_count - 1)
    def _():
        greet((t + 1, s))

    def block(row, column):
        return geometry.at[pl.ds((row * 8 + column) * COMPS, COMPS)]

    base = (8 + s) * COMPS
    pad = jnp.zeros((own, LANES - nodes), F32)
    for c in range(3):
        geometry[base + c] = jnp.concatenate([positions[c], pad + FAR_AWAY], axis=1)
        geometry[base + 3 + c] = jnp.concatenate([density[c] * weights[...], pad], axis=1)
    lists[s] = jnp.concatenate([near[...], jnp.full((own, 120), -1, jnp.int32)], axis=1)

    lane = lax.broadcasted_iota(jnp.int32, (16, 128), 1)
    spread = jnp.zeros((16, 128), F32)
    for j in range(own):
        product = basis[j, 0].astype(F32) * density[0, j : j + 1, :]
        for c in range(1, 3):
            product = product + basis[j, c].astype(F32) * density[c, j : j + 1, :]
        value = jnp.sum(product, axis=1, keepdims=True)
        spread = jnp.where(lane == (t % 4) * 32 + s * 4 + j, value, spread)
    coef_mine[...] = spread.astype(BF16)

    pl.semaphore_wait(
        barrier,
        7
        + 7
        + jnp.where(loops_back, 3, 4)
        + jnp.where(t > 0, 1, 0)
        + jnp.where(t < t_count - 1, 1, 0),
    )

    started = []

    def first_copy(u):
        return remote(
            coef_mine,
            coef_relay.at[t % 4],
            first_send.at[u],
            first_recv.at[t % 4],
            (u * 8 + s, quarter),
        )

    for u in range(4):
        away = jnp.logical_not(jnp.logical_and(loops_back, u == group))

        @pl.when(away)
        def _():
            first_copy(u).start()

        @pl.when(jnp.logical_not(away))
        def _():
            coef_relay[t % 4] = coef_mine[...]

    def row_copy(index, column, device):
        return remote(
            block(1, column),
            block(1, column),
            row_send.at[index],
            row_recv.at[index],
            device,
        )

    def right(column):
        return (column + 2) % 8

    def left(column):
        return (column + 6) % 8

    def halo_copy(side, index, column):
        return remote(
            block(1, column),
            block(2 * side, column),
            halo_send.at[side * 8 + index],
            halo_recv.at[side * 8 + index],
            (t + 1 - 2 * side, s),
        )

    def halo_start(index, column):
        @pl.when(t < t_count - 1)
        def _():
            halo_copy(0, index, column).start()

        @pl.when(t > 0)
        def _():
            halo_copy(1, index, column).start()

    partner = s + 1 - 2 * z
    copies = {}

    def row_start(index, column, device):
        copies[index] = row_copy(index, column, device)
        copies[index].start()

    def ring_start(turn, column):
        row_start(1 + 3 * turn, column, (t, right(s)))
        row_start(2 + 3 * turn, column, (t, left(s)))
        halo_start(4 * turn, column)

    def ring_forward(turn, column):
        copies[1 + 3 * turn].wait_recv()
        copies[2 + 3 * turn].wait_recv()
        even = t % 2 == 0
        from_left = left(column)
        from_right = right(column)
        passed = jnp.where(even, from_left, from_right)
        row_start(3 + 3 * turn, passed, (t, jnp.where(even, right(s), left(s))))
        halo_start(4 * turn + 1, from_left)
        halo_start(4 * turn + 2, from_right)

    def ring_end(turn, column):
        copies[3 + 3 * turn].wait_recv()
        halo_start(4 * turn + 3, (column + 4) % 8)

    row_start(0, s, (t, partner))
    ring_start(0, s)

    def list_copy(step):
        return remote(
            lists.at[s],
            lists.at[s],
            list_send.at[step - 1],
            list_recv.at[step - 1],
            (t, (s + step) % 8),
        )

    list_copies = [list_copy(step) for step in range(1, 8)]
    for copy in list_copies:
        copy.start()

    for part in range(4):

        @pl.when(jnp.logical_not(jnp.logical_and(loops_back, part == t % 4)))
        def _():
            remote(
                coef_mine,
                coef_relay.at[part],
                first_send.at[part],
                first_recv.at[part],
                (4 * s + part, place),
            ).wait_recv()

    total = coef_relay[0].astype(F32)
    for part in range(1, 4):
        total = total + coef_relay[part].astype(F32)
    coef_sum[...] = total.astype(BF16)
    second_copies = []
    for step in range(1, 8):
        copy = remote(
            coef_sum,
            coef_parts.at[step - 1],
            second_send.at[step - 1],
            second_recv.at[step - 1],
            (group * 8 + (place + step) % 8, s),
        )
        copy.start()
        second_copies.append(copy)

    ring_forward(0, s)
    copies[0].wait_recv()
    ring_start(1, partner)

    for copy in list_copies:
        copy.wait_recv()
    rows = 8 * own
    listed = lists[...].reshape(rows, 128)
    ids = s * 128 + lax.broadcasted_iota(jnp.int32, (rows, 128), 1)
    hit = ids == t * rows + lax.broadcasted_iota(jnp.int32, (rows, 128), 0)
    for k in range(near.shape[1]):
        hit = jnp.logical_or(hit, ids == listed[:, k : k + 1])
    mask[...] = jnp.where(hit, F32(0.0), F32(1.0))
    for copy in second_copies:
        copy.wait_recv()
    coef = coef_sum[...].astype(F32)
    for step in range(1, 8):
        coef = coef + coef_parts[step - 1].astype(F32)
    load.wait()

    def fold(i, _):
        kept = coef * mask[pl.ds(i, 1), :]
        product = held[i].astype(F32) * kept[None]
        folded[pl.ds(pl.multiple_of(i * 16, 16), 16), :] = jnp.sum(product, axis=1)
        return 0

    lax.fori_loop(0, rows, fold, 0)
    for q in range(4):
        turned = folded[q * 128 : (q + 1) * 128, :].T
        far_mine[q] = jnp.broadcast_to(jnp.sum(turned, axis=0, keepdims=True), (8, 128))
    far_copies = []
    for step in range(1, 8):
        other = (s + step) % 8
        copy = remote(
            far_mine.at[other // 2],
            far_parts.at[step - 1],
            far_send.at[step - 1],
            far_recv.at[step - 1],
            (t, other),
        )
        copy.start()
        far_copies.append(copy)

    ring_end(0, s)
    ring_forward(1, partner)
    ring_end(1, partner)

    for copy in far_copies:
        copy.wait_recv()
    w = far_mine[s // 2]
    for step in range(1, 8):
        w = w + far_parts[step - 1]
    coupled[...] = jnp.where(s % 2 == 1, pltpu.roll(w, 64, 1), w)

    for side in range(2):
        there = t > 0 if side == 0 else t < t_count - 1
        mine = t < t_count - 1 if side == 0 else t > 0

        @pl.when(there)
        def _():
            for index in range(8):
                start = s if index < 4 else partner
                column = (start + (0, 6, 2, 4)[index % 4]) % 8
                remote(
                    block(1, column),
                    block(2 * side, column),
                    halo_send.at[side * 8 + index],
                    halo_recv.at[side * 8 + index],
                    (t, s),
                ).wait_recv()

        @pl.when(mine)
        def _():
            for index in range(8):
                start = s if index < 4 else partner
                halo_copy(side, index, (start + (0, 6, 2, 4)[index % 4]) % 8).wait_send()

    for copy in list_copies + second_copies + far_copies + list(copies.values()):
        copy.wait_send()
    for u in range(4):

        @pl.when(jnp.logical_not(jnp.logical_and(loops_back, u == group)))
        def _():
            first_copy(u).wait_send()


def split(value):
    high = value.astype(BF16).astype(F32)
    rest = value - high
    middle = rest.astype(BF16).astype(F32)
    return high, middle, rest - middle


def velocity_kernel(
    nodes,
    near,
    geometry,
    coupled,
    basis,
    out,
    used,
    centre,
    features,
    spread0,
    spread1,
    moment0,
    moment1,
    kernel0,
    kernel1,
    total,
    slots,
    worst,
    columns,
):
    t = lax.axis_index("tgt")
    s = lax.axis_index("src")
    own = out.shape[1]
    per_body = near.shape[1]
    first_id = (t - 1) * 32
    own_base = (8 + s) * COMPS
    total[...] = jnp.zeros_like(total)
    moment1[...] = jnp.zeros_like(moment1)
    kernel1[...] = jnp.zeros_like(kernel1)
    worst[...] = jnp.full_like(worst, -1.0)
    for i in range(own):
        for c in range(COMPS):
            slots[i * COMPS + c] = jnp.full((8, LANES), FAR_AWAY if c < 3 else 0.0, F32)

    def listing(k, n):
        active = near[k // per_body, k % per_body] >= 0

        @pl.when(active)
        def _():
            used[n] = k

        return n + jnp.where(active, 1, 0)

    n = lax.fori_loop(0, own * per_body, listing, jnp.int32(0))
    used[n] = 0
    used[n + 1] = 0

    inside = lax.broadcasted_iota(jnp.int32, (own, LANES), 1) < nodes
    radius = jnp.zeros((own, LANES), F32)
    for c in range(3):
        value = geometry[own_base + c]
        mean = jnp.sum(jnp.where(inside, value, 0.0), axis=1, keepdims=True) / nodes
        centre[c] = jnp.broadcast_to(mean, (own, LANES))
        offset = jnp.where(inside, value - mean, 0.0)
        radius = radius + offset * offset
    largest = jnp.max(radius, axis=1, keepdims=True)
    centre[3] = jnp.broadcast_to(jnp.sqrt(largest), (own, LANES))

    def target_rows(i):
        return [geometry[own_base + c, i : i + 1, :] - centre[c, i : i + 1, :] for c in range(3)]

    for i in range(own):
        x = target_rows(i)
        square = x[0] * x[0] + x[1] * x[1] + x[2] * x[2]
        one = jnp.ones_like(square)
        zero = jnp.zeros_like(square)
        parts = split(jnp.concatenate(x + [one, square, zero, zero, zero], axis=0))
        empty = jnp.zeros((8, LANES), F32)
        stack = []
        for part in parts:
            stack += [part, part, part, empty]
        features[i] = jnp.concatenate(stack, axis=0).astype(BF16)[:, :MAIN]

    sub = lax.broadcasted_iota(jnp.int32, (8, LANES), 0)

    def pair(m):
        k = used[m]
        body = near[k // per_body, k % per_body] - first_id
        return k // per_body, k % per_body, (body // 4) * COMPS, body % 4

    def source_stage(m, spread, moment):
        i, slot, base, place = pair(m)
        raw = [geometry[base + c, pl.ds(place, 1), :] for c in range(COMPS)]
        live = jnp.where(m < n, F32(1.0), F32(0.0))

        for c in range(COMPS):
            slots[i * COMPS + c, pl.ds(slot, 1), :] = raw[c]

        y = [
            jnp.broadcast_to(raw[c] - centre[c, pl.ds(i, 1), :], (8, LANES)) for c in range(3)
        ]
        w = [jnp.broadcast_to(raw[3 + c], (8, LANES)) for c in range(3)]
        square = y[0] * y[0] + y[1] * y[1] + y[2] * y[2]
        reach = jnp.sqrt(square)
        size = jnp.broadcast_to(centre[3, pl.ds(i, 1), :], (8, LANES))
        ratio = (reach + size) - MOST_RATIO * jnp.maximum(reach - size, LEAST_GAP)
        worst[...] = jnp.maximum(worst[...], ratio)
        along = y[0] * w[0] + y[1] * w[1] + y[2] * w[2]
        left = jnp.where(
            sub == 0,
            -2.0 * y[0],
            jnp.where(
                sub == 1,
                -2.0 * y[1],
                jnp.where(
                    sub == 2,
                    -2.0 * y[2],
                    jnp.where(sub == 3, square, jnp.where(sub == 4, F32(1.0), F32(0.0))),
                ),
            ),
        )
        empty = jnp.zeros((8, LANES), F32)
        third = jnp.concatenate(list(split(left)) + [empty], axis=0).astype(BF16)[:, :ROWS]
        spread[...] = jnp.concatenate([third, third, third], axis=0)
        quad = sub % 4
        plain = live * jnp.where(
            quad == 0, w[0], jnp.where(quad == 1, w[1], jnp.where(quad == 2, w[2], along))
        )
        once = plain * jnp.where(sub < 4, y[0], y[1])
        twice = plain * jnp.where(sub < 4, y[2], square)
        parts = [split(value) for value in (plain, once, twice)]
        stack = [parts[q][p] for p in range(3) for q in range(3)] + [empty]
        moment[...] = jnp.concatenate(stack, axis=0).astype(BF16)[:, :ROWS]

    def kernel_chunk(m, spread, kernel, low, high):
        i = used[m] // per_body
        squared = lax.dot_general(
            spread[:, low:high],
            features[i],
            (((0,), (0,)), ((), ())),
            preferred_element_type=F32,
        )
        inverse = lax.rsqrt(squared)
        kernel[low:high] = (inverse * inverse * inverse).astype(BF16)

    def moment_chunk(m, kernel, moment, low, high):
        i = used[jnp.maximum(m, 0)] // per_body
        total[i] += jnp.dot(moment[:, low:high], kernel[low:high], preferred_element_type=F32)

    cuts = (0, 208, 432, ROWS)

    def turn(q, _):
        first = (kernel0, moment0, spread0)
        second = (kernel1, moment1, spread1)
        for e, (mine, other) in enumerate(((first, second), (second, first))):
            m = 2 * q + e
            for low, high in zip(cuts[:-1], cuts[1:]):
                kernel_chunk(m, mine[2], mine[0], low, high)
                moment_chunk(m - 1, other[0], other[1], low, high)
            source_stage(m + 1, other[2], other[1])
        return 0

    halves = (n + 1) // 2
    source_stage(0, spread0, moment0)
    lax.fori_loop(0, halves, turn, 0)
    moment_chunk(2 * halves - 1, kernel1, moment1, 0, ROWS)

    row8 = lax.broadcasted_iota(jnp.int32, (8, 128), 0)
    lane8 = lax.broadcasted_iota(jnp.int32, (8, 128), 1)
    diagonal = jnp.where(lane8 // 16 == row8, coupled[...], 0.0).astype(BF16)[:, :64]
    far = []
    for c in range(3):
        flat = jnp.concatenate([basis[i, c] for i in range(own)], axis=0)
        far.append(jnp.dot(diagonal, flat, preferred_element_type=F32))

    for i in range(own):
        y = [slots[i * COMPS + c] for c in range(3)]
        w = [slots[i * COMPS + 3 + c] for c in range(3)]
        sums = [[], [], []]
        for node in range(MAIN, nodes):
            d = [geometry[own_base + c, i : i + 1, node : node + 1] - y[c] for c in range(3)]
            inverse = lax.rsqrt(d[0] * d[0] + d[1] * d[1] + d[2] * d[2])
            pull = (d[0] * w[0] + d[1] * w[1] + d[2] * w[2]) * (inverse * inverse * inverse)
            for c in range(3):
                value = w[c] * inverse + d[c] * pull
                folded = jnp.sum(value, axis=0, keepdims=True)
                sums[c].append(jnp.sum(folded, axis=1, keepdims=True))
        for c in range(3):
            tail = jnp.concatenate(sums[c], axis=1)
            out[c, i : i + 1, MAIN:nodes] = tail + far[c][i : i + 1, MAIN:nodes]

    crowded = jnp.max(worst[...]) > 0.0

    @pl.when(jnp.logical_not(crowded))
    def _():
        for i in range(own):
            at = total[i]
            g = at[0:24] + at[24:48] + at[48:72]
            x = [value[:, :MAIN] for value in target_rows(i)]
            plain = [g[k : k + 1] for k in range(3)]
            first = [[g[b + k : b + k + 1] for k in range(3)] for b in (8, 12, 16)]
            along = [g[b + 3 : b + 4] for b in (3 - 3, 8, 12, 16)]
            second = [g[20 + k : 21 + k] for k in range(3)]
            square = x[0] * x[0] + x[1] * x[1] + x[2] * x[2]
            inner = x[0] * plain[0] + x[1] * plain[1] + x[2] * plain[2] - along[0]
            for c in range(3):
                u = square * plain[c] + second[c] + along[1 + c] + x[c] * inner
                for k in range(3):
                    u = u - x[k] * (2.0 * first[k][c] + first[c][k])
                out[c, i : i + 1, :MAIN] = u + far[c][i : i + 1, :MAIN]

    @pl.when(crowded)
    def _():
        for i in range(own):
            for c in range(3):
                out[c, i : i + 1, :MAIN] = far[c][i : i + 1, :MAIN]

        def direct(m, _):
            i, slot, base, place = pair(m)
            rows = [geometry[base + c, pl.ds(place, 1), :] for c in range(COMPS)]
            empty = jnp.zeros((2, LANES), F32)
            columns[...] = jnp.concatenate(rows + [empty], axis=0).T
            x = [geometry[own_base + c, pl.ds(i, 1), :MAIN] for c in range(3)]

            def eight(q, sums):
                block = columns[pl.ds(pl.multiple_of(q * 8, 8), 8), :]
                d = [x[c] - block[:, c : c + 1] for c in range(3)]
                w = [block[:, 3 + c : 4 + c] for c in range(3)]
                inverse = lax.rsqrt(d[0] * d[0] + d[1] * d[1] + d[2] * d[2])
                pull = d[0] * w[0] + d[1] * w[1] + d[2] * w[2]
                pull = pull * (inverse * inverse * inverse)
                return tuple(sums[c] + (w[c] * inverse + d[c] * pull) for c in range(3))

            start = tuple(jnp.zeros((8, MAIN), F32) for _ in range(3))
            sums = lax.fori_loop(0, ROWS // 8, eight, start)
            for c in range(3):
                out[c, pl.ds(i, 1), :MAIN] += jnp.sum(sums[c], axis=0, keepdims=True)
            return 0

        lax.fori_loop(0, n, direct, 0)


def local(positions, weights, density, near_source, couplings, source_basis, target_basis):
    own, _, nodes = positions.shape
    vmem = pl.BlockSpec(memory_space=pltpu.VMEM)
    dma = pltpu.SemaphoreType.DMA
    turned = (1, 0, 2)
    geometry, coupled = pl.pallas_call(
        functools.partial(exchange_kernel, nodes),
        out_shape=(
            jax.ShapeDtypeStruct((24 * COMPS, own, LANES), F32),
            jax.ShapeDtypeStruct((8, 128), F32),
        ),
        in_specs=[vmem] * 4 + [pl.BlockSpec(memory_space=pl.ANY), vmem],
        out_specs=(vmem, vmem),
        scratch_shapes=[
            pltpu.VMEM((32, 16, 16, 128), BF16),
            pltpu.VMEM((16, 128), BF16),
            pltpu.VMEM((4, 16, 128), BF16),
            pltpu.VMEM((16, 128), BF16),
            pltpu.VMEM((7, 16, 128), BF16),
            pltpu.VMEM((8, own, 128), jnp.int32),
            pltpu.VMEM((32, 128), F32),
            pltpu.VMEM((512, 128), F32),
            pltpu.VMEM((4, 8, 128), F32),
            pltpu.VMEM((7, 8, 128), F32),
            dma,
            dma((7,)),
            dma((7,)),
            dma((4,)),
            dma((4,)),
            dma((7,)),
            dma((7,)),
            dma((7,)),
            dma((7,)),
            dma((7,)),
            dma((7,)),
            dma((16,)),
            dma((16,)),
        ],
        compiler_params=pltpu.CompilerParams(
            collective_id=0, has_side_effects=True, vmem_limit_bytes=32 * 2**20
        ),
        name="exchange",
    )(
        positions.transpose(turned),
        weights,
        density.transpose(turned),
        near_source,
        couplings.transpose(0, 2, 3, 1),
        source_basis.transpose(0, 2, 1, 3),
    )
    out = pl.pallas_call(
        functools.partial(velocity_kernel, nodes),
        out_shape=jax.ShapeDtypeStruct((3, own, nodes), F32),
        in_specs=[pl.BlockSpec(memory_space=pltpu.SMEM)] + [vmem] * 3,
        out_specs=vmem,
        scratch_shapes=[
            pltpu.SMEM((40,), jnp.int32),
            pltpu.VMEM((4, own, LANES), F32),
            pltpu.VMEM((own, 96, MAIN), BF16),
            pltpu.VMEM((96, ROWS), BF16),
            pltpu.VMEM((96, ROWS), BF16),
            pltpu.VMEM((80, ROWS), BF16),
            pltpu.VMEM((80, ROWS), BF16),
            pltpu.VMEM((ROWS, MAIN), BF16),
            pltpu.VMEM((ROWS, MAIN), BF16),
            pltpu.VMEM((own, 80, MAIN), F32),
            pltpu.VMEM((own * COMPS, 8, LANES), F32),
            pltpu.VMEM((8, LANES), F32),
            pltpu.VMEM((LANES, 8), F32),
        ],
        compiler_params=pltpu.CompilerParams(vmem_limit_bytes=32 * 2**20),
        name="velocity",
    )(near_source, geometry, coupled, target_basis.transpose(0, 2, 1, 3))
    return out.transpose(turned)


def solution(mesh):
    placed = (
        P(("tgt", "src"), None, None),
        P(("tgt", "src"), None),
        P(("tgt", "src"), None, None),
        P(("tgt", "src"), None),
        P("tgt", "src", None, None),
        P(("tgt", "src"), None, None, None),
        P(("tgt", "src"), None, None, None),
    )
    return jax.shard_map(
        local, mesh=mesh, in_specs=placed, out_specs=P(("tgt", "src"), None, None), check_vma=False
    )
```

time: 1290 us -> 52.5 us (0.04)
  blocking collectives: 884 us -> 0 us
  other arithmetic: 199 us -> 0 us
  waiting for transfers between devices: 104 us -> 0 us
  local copies, waits for them, and re-layouts: 73.2 us -> 5.48 us
  Pallas kernels: 0 us -> 46.7 us
  between operations: 14.1 us -> 0.02 us
    all_gather x3 -> x0, blocking collectives: 832 us -> none  [the longest x1 736 us: local(): lax.all_gather(coef.astype(jnp.bfloat16), ('tgt', 'src'), axis=0, tiled=T...]
    reduce_sum x8 -> x0, other arithmetic: 180 us -> none  [stokeslet(): first = jnp.sum(weighted[0][None, :] * inverse + delta_x * pull, axis=1)]
    unnamed x2 -> x0, waiting for transfers between devices: 104 us -> none
    unnamed x1 -> x0, blocking collectives: 52.5 us -> none
    pallas_call x0 -> x2, Pallas kernels: none -> 46.7 us  [the longest x1 29.9 us: local(): pl.pallas_call(functools.partial(exchange_kernel, nodes), out_shape=(jax....]
    another operation x25 -> x0, local copies, waits for them, and re-layouts: 19.3 us -> none  [the longest x24 19.3 us: stokeslet(): return jnp.stack([first, second, third], 0)]
    gather x8 -> x0, local copies, waits for them, and re-layouts: 17.7 us -> none  [evaluate(): sources_now = near_pack[picked]]
  transfers between devices with their start and end apart: 3 -> 0, of which waited for: 1 -> 0; matrix products, arithmetic and copies ran while one was open for 1% -> 0% of each run, Pallas kernels for 0% -> 0%
where the time goes in v1:
time: 52.5 us; the launch traced here: 52.2 us
  Pallas kernels  46.7 us (89%)
  local copies, waits for them, and re-layouts  5.48 us (10%)
    pallas_call x1, Pallas kernels, local(): pl.pallas_call(functools.partial(exchange_kernel, nodes), out_shape=(jax....  29.9 us
    pallas_call x1, Pallas kernels, local(): pl.pallas_call(functools.partial(velocity_kernel, nodes), out_shape=jax.S...  16.8 us
    unnamed x14, local copies, waits for them, and re-layouts  5.48 us

profile of v1, /device:TPU:64, one launch (start us, length us, event | category | flops | bytes accessed | tf_op | source)
XLA Modules:
  0.0 52.2 jit_solution(15151126624603485304)
XLA Ops:
  0.0 0.0 copy-start
  0.0 1.6 %copy-done = bf16[32,128,16,16]{1,3,2,0:T(8,128)(2,1)S(1)} copy-done((bf16[32,128,16,16]{1,3,2,0:T(8,128)(2,1)S(1)}, bf16[32,128,16,16]{1,3,2,0:T(8,128)(2,1)}, u32[]{:S(2)}) %copy-start) | copy-done | bytes 2097176
  1.6 0.0 copy-start.2
  1.6 1.0 %copy-done.2 = bf16[4,16,3,642]{3,1,2,0:T(8,128)(2,1)S(1)} copy-done((bf16[4,16,3,642]{3,1,2,0:T(8,128)(2,1)S(1)}, bf16[4,16,3,642]{3,1,2,0:T(8,128)(2,1)}, u32[]{:S(2)}) %copy-start.2) | copy-done | bytes 246552
  2.6 0.0 copy-start.3
  2.6 0.8 %copy-done.3 = f32[4,3,642]{2,0,1:T(4,128)S(1)} copy-done((f32[4,3,642]{2,0,1:T(4,128)S(1)}, f32[4,3,642]{2,0,1:T(4,128)}, u32[]{:S(2)}) %copy-start.3) | copy-done | bytes 30840
  3.3 0.0 copy-start.4
  3.3 0.8 %copy-done.4 = f32[4,3,642]{2,0,1:T(4,128)S(1)} copy-done((f32[4,3,642]{2,0,1:T(4,128)S(1)}, f32[4,3,642]{2,0,1:T(4,128)}, u32[]{:S(2)}) %copy-start.4) | copy-done | bytes 30840
  4.1 0.0 copy-start.5
  4.1 0.7 %copy-done.5 = f32[4,642]{1,0:T(4,128)S(1)} copy-done((f32[4,642]{1,0:T(4,128)S(1)}, f32[4,642]{1,0:T(4,128)}, u32[]{:S(2)}) %copy-start.5) | copy-done | bytes 10296
  4.8 0.0 copy-start.6
  4.8 0.7 %copy-done.6 = s32[4,8]{1,0:T(4,128)S(1)} copy-done((s32[4,8]{1,0:T(4,128)S(1)}, s32[4,8]{1,0:T(4,128)}, u32[]{:S(2)}) %copy-start.6) | copy-done | bytes 152
  5.5 0.0 copy-start.1
  5.5 29.9 %exchange.1 = (f32[144,4,768]{2,1,0:T(4,128)S(1)}, f32[8,128]{1,0:T(8,128)S(1)}) custom-call(f32[3,4,642]{2,1,0:T(4,128)S(1)} %bitcast.9, f32[4,642]{1,0:T(4,128)S(1)} %copy-done.5, f32[3,4,642]{2,1,0:T(4,128)S(1)} %bitcast.10, s32[4,8]{1,0:T(4,128)S(1)} %copy-done.6, bf16[32,16,16,128]{3,2,1,0:T(8,128)(2,1)S(1)} %bitcast.6, bf16[4,3,16,642]{3,2,1,0:T(8,128)(2,1)S(1)} %bitcast.8), custom_call_target="tpu_custom_call" | custom-call | tf_op jit(solution)/shard_map/exchange/pallas_call | solution.py:588
  35.4 0.0 copy-done.1
  35.4 16.8 %velocity.1 = f32[3,4,642]{2,1,0:T(4,128)} custom-call(s32[4,8]{1,0:T(4,128)S(1)} %copy-done.6, f32[144,4,768]{2,1,0:T(4,128)S(1)} %get-tuple-element.7.geometry, f32[8,128]{1,0:T(8,128)S(1)} %get-tuple-element.8.coupled, bf16[4,3,16,642]{3,2,1,0:T(8,128)(2,1)S(1)} %bitcast.7), custom_call_target="tpu_custom_call" | custom-call | tf_op jit(solution)/shard_map/velocity/pallas_call | solution.py:633
Async XLA Ops:
  0.0 1.6 %copy-start = (bf16[32,128,16,16]{1,3,2,0:T(8,128)(2,1)S(1)}, bf16[32,128,16,16]{1,3,2,0:T(8,128)(2,1)}, u32[]{:S(2)}) copy-start(bf16[32,128,16,16]{1,3,2,0:T(8,128)(2,1)} %param.11) | copy-start | bytes 6291460
  1.6 1.0 %copy-start.2 = (bf16[4,16,3,642]{3,1,2,0:T(8,128)(2,1)S(1)}, bf16[4,16,3,642]{3,1,2,0:T(8,128)(2,1)}, u32[]{:S(2)}) copy-start(bf16[4,16,3,642]{3,1,2,0:T(8,128)(2,1)} %param.12) | copy-start | bytes 739588
  2.6 0.8 %copy-start.3 = (f32[4,3,642]{2,0,1:T(4,128)S(1)}, f32[4,3,642]{2,0,1:T(4,128)}, u32[]{:S(2)}) copy-start(f32[4,3,642]{2,0,1:T(4,128)} %param.7) | copy-start | bytes 92452
  3.3 0.8 %copy-start.4 = (f32[4,3,642]{2,0,1:T(4,128)S(1)}, f32[4,3,642]{2,0,1:T(4,128)}, u32[]{:S(2)}) copy-start(f32[4,3,642]{2,0,1:T(4,128)} %param.9) | copy-start | bytes 92452
  4.1 0.7 %copy-start.5 = (f32[4,642]{1,0:T(4,128)S(1)}, f32[4,642]{1,0:T(4,128)}, u32[]{:S(2)}) copy-start(f32[4,642]{1,0:T(4,128)} %weights.1) | copy-start | bytes 30820
  4.8 0.7 %copy-start.6 = (s32[4,8]{1,0:T(4,128)S(1)}, s32[4,8]{1,0:T(4,128)}, u32[]{:S(2)}) copy-start(s32[4,8]{1,0:T(4,128)} %near.3) | copy-start | bytes 388
  5.5 29.9 %copy-start.1 = (bf16[4,16,3,642]{3,1,2,0:T(8,128)(2,1)S(1)}, bf16[4,16,3,642]{3,1,2,0:T(8,128)(2,1)}, u32[]{:S(2)}) copy-start(bf16[4,16,3,642]{3,1,2,0:T(8,128)(2,1)} %param.13) | copy-start | bytes 739588

commit v2 on v1

v2 whole, which is shorter than its diff:
```python
import functools
import jax
import jax.numpy as jnp
from jax import lax
from jax.experimental import pallas as pl
from jax.experimental.pallas import tpu as pltpu
from jax.sharding import PartitionSpec as P

F32 = jnp.float32
BF16 = jnp.bfloat16
LANES = 768
ROWS = 656
MAIN = 640
COMPS = 6
FAR_AWAY = 1000.0
LEAST_GAP = 0.1
MOST_RATIO = 70.0
EARLY = 3
CUTS = (0, 208, 432, ROWS)
VMEM_BYTES = 58 * 2**20
MESH = pl.DeviceIdType.MESH


def remote(source, target, send, recv, device):
    return pltpu.make_async_remote_copy(
        src_ref=source,
        dst_ref=target,
        send_sem=send,
        recv_sem=recv,
        device_id=device,
        device_id_type=MESH,
    )


def split(value):
    high = value.astype(BF16).astype(F32)
    rest = value - high
    middle = rest.astype(BF16).astype(F32)
    return high, middle, rest - middle


def target_stage(nodes, own, load, centre, features):
    inside = lax.broadcasted_iota(jnp.int32, (own, LANES), 1) < nodes
    radius = jnp.zeros((own, LANES), F32)
    offsets = []
    for c in range(3):
        value = load(c)
        mean = jnp.sum(jnp.where(inside, value, 0.0), axis=1, keepdims=True) / nodes
        centre[c] = jnp.broadcast_to(mean, (own, LANES))
        offset = jnp.where(inside, value - mean, 0.0)
        offsets.append(offset)
        radius = radius + offset * offset
    largest = jnp.max(radius, axis=1, keepdims=True)
    centre[3] = jnp.broadcast_to(jnp.sqrt(largest), (own, LANES))
    for i in range(own):
        x = [offset[i : i + 1, :] for offset in offsets]
        square = radius[i : i + 1, :]
        one = jnp.ones_like(square)
        zero = jnp.zeros_like(square)
        parts = split(jnp.concatenate(x + [one, square, zero, zero, zero], axis=0))
        empty = jnp.zeros((8, LANES), F32)
        stack = []
        for part in parts:
            stack += [part, part, part, empty]
        features[i] = jnp.concatenate(stack, axis=0).astype(BF16)[:, :MAIN]


def source_stage(raw, i, live, centre, worst, spread, moment):
    sub = lax.broadcasted_iota(jnp.int32, (8, LANES), 0)
    y = [jnp.broadcast_to(raw[c] - centre[c, pl.ds(i, 1), :], (8, LANES)) for c in range(3)]
    w = [jnp.broadcast_to(raw[3 + c], (8, LANES)) for c in range(3)]
    square = y[0] * y[0] + y[1] * y[1] + y[2] * y[2]
    reach = jnp.sqrt(square)
    size = jnp.broadcast_to(centre[3, pl.ds(i, 1), :], (8, LANES))
    ratio = (reach + size) - MOST_RATIO * jnp.maximum(reach - size, LEAST_GAP)
    worst[...] = jnp.maximum(worst[...], ratio)
    along = y[0] * w[0] + y[1] * w[1] + y[2] * w[2]
    left = jnp.where(
        sub == 0,
        -2.0 * y[0],
        jnp.where(
            sub == 1,
            -2.0 * y[1],
            jnp.where(
                sub == 2,
                -2.0 * y[2],
                jnp.where(sub == 3, square, jnp.where(sub == 4, F32(1.0), F32(0.0))),
            ),
        ),
    )
    empty = jnp.zeros((8, LANES), F32)
    third = jnp.concatenate(list(split(left)) + [empty], axis=0).astype(BF16)[:, :ROWS]
    spread[...] = jnp.concatenate([third, third, third], axis=0)
    quad = sub % 4
    plain = live * jnp.where(
        quad == 0, w[0], jnp.where(quad == 1, w[1], jnp.where(quad == 2, w[2], along))
    )
    once = plain * jnp.where(sub < 4, y[0], y[1])
    twice = plain * jnp.where(sub < 4, y[2], square)
    parts = [split(value) for value in (plain, once, twice)]
    stack = [parts[q][p] for p in range(3) for q in range(3)] + [empty]
    moment[...] = jnp.concatenate(stack, axis=0).astype(BF16)[:, :ROWS]


def kernel_chunk(features, spread, kernel, low, high):
    squared = lax.dot_general(
        spread[:, low:high], features, (((0,), (0,)), ((), ())), preferred_element_type=F32
    )
    inverse = lax.rsqrt(squared)
    kernel[low:high] = (inverse * inverse * inverse).astype(BF16)


def moment_chunk(kernel, moment, low, high):
    return jnp.dot(moment[:, low:high], kernel[low:high], preferred_element_type=F32)


def near_pairs(count, target_of, source, features, total, first, second):
    def turn(q, _):
        for e, (mine, other) in enumerate(((first, second), (second, first))):
            m = 2 * q + e
            for low, high in zip(CUTS[:-1], CUTS[1:]):
                kernel_chunk(features[target_of(m)], mine[2], mine[0], low, high)
                total[target_of(m - 1)] += moment_chunk(other[0], other[1], low, high)
            source(m + 1, other[2], other[1])
        return 0

    halves = (count + 1) // 2
    source(0, first[2], first[1])
    lax.fori_loop(0, halves, turn, 0)
    total[target_of(2 * halves - 1)] += moment_chunk(second[0], second[1], 0, ROWS)


def exchange_kernel(
    nodes,
    positions_in,
    weights_in,
    density_in,
    near_in,
    couplings_in,
    basis_in,
    row_out,
    halo_out,
    coupled_out,
    total_out,
    worst_out,
    slots_out,
    row_geometry,
    coupled,
    total,
    worst,
    slots,
    positions,
    weights,
    density,
    near,
    near_scalar,
    held,
    basis,
    coef_mine,
    coef_parts,
    lists,
    mask,
    folded,
    far_mine,
    far_parts,
    chosen,
    centre,
    features,
    spread0,
    spread1,
    moment0,
    moment1,
    kernel0,
    kernel1,
    load_sem,
    store_sem,
    list_send,
    list_recv,
    coef_send,
    coef_recv,
    far_send,
    far_recv,
    row_send,
    row_recv,
    halo_send,
    halo_recv,
):
    t = lax.axis_index("tgt")
    s = lax.axis_index("src")
    t_count = lax.axis_size("tgt")
    quarter = t // 4
    own = positions.shape[1]
    slot_count = near.shape[1]
    loops_back = quarter == s
    partner = s + 1 - 2 * (s % 2)

    loads = [
        pltpu.make_async_copy(source, target, load_sem.at[index])
        for index, (source, target) in enumerate(
            (
                (positions_in, positions),
                (weights_in, weights),
                (density_in, density),
                (near_in, near),
                (near_in, near_scalar),
                (basis_in, basis),
                (couplings_in, held),
            )
        )
    ]
    for load in loads:
        load.start()

    barrier = pltpu.get_barrier_semaphore()

    def greet(device):
        pl.semaphore_signal(barrier, inc=1, device_id=device, device_id_type=MESH)

    for step in range(1, 8):
        greet((t, (s + step) % 8))

    def greet_source(k, _):
        @pl.when(jnp.logical_not(jnp.logical_and(loops_back, k == (t % 4) * 8 + s)))
        def _():
            greet((4 * s + k // 8, k % 8))

        return 0

    lax.fori_loop(0, t_count, greet_source, 0)

    @pl.when(t > 0)
    def _():
        greet((t - 1, s))

    @pl.when(t < t_count - 1)
    def _():
        greet((t + 1, s))

    def block(column):
        return row_geometry.at[pl.ds(column * COMPS, COMPS)]

    for load in loads[:4]:
        load.wait()
    pad = jnp.zeros((own, LANES - nodes), F32)
    for c in range(3):
        row_geometry[s * COMPS + c] = jnp.concatenate([positions[c], pad + FAR_AWAY], axis=1)
        row_geometry[s * COMPS + 3 + c] = jnp.concatenate(
            [density[c] * weights[...], pad], axis=1
        )
    lists[s] = jnp.concatenate([near[...], jnp.full((own, 120), -1, jnp.int32)], axis=1)

    loads[5].wait()
    lane = lax.broadcasted_iota(jnp.int32, (16, 128), 1)
    spread = jnp.zeros((16, 128), F32)
    for j in range(own):
        product = basis[j, 0].astype(F32) * density[0, j : j + 1, :]
        for c in range(1, 3):
            product = product + basis[j, c].astype(F32) * density[c, j : j + 1, :]
        value = jnp.sum(product, axis=1, keepdims=True)
        spread = jnp.where(lane == (t % 4) * 32 + s * 4 + j, value, spread)
    coef_mine[...] = spread.astype(BF16)

    pl.semaphore_wait(
        barrier,
        7
        + t_count
        - jnp.where(loops_back, 1, 0)
        + jnp.where(t > 0, 1, 0)
        + jnp.where(t < t_count - 1, 1, 0),
    )

    def row_copy(index, column, device):
        return remote(
            block(column), block(column), row_send.at[index], row_recv.at[index], (t, device)
        )

    def halo_copy(side, index, column):
        return remote(
            block(column),
            halo_out.at[pl.ds((side * 8 + column) * COMPS, COMPS)],
            halo_send.at[side * 8 + index],
            halo_recv.at[side * 8 + index],
            (t + 1 - 2 * side, s),
        )

    def halo_start(index, column):
        @pl.when(t < t_count - 1)
        def _():
            halo_copy(0, index, column).start()

        @pl.when(t > 0)
        def _():
            halo_copy(1, index, column).start()

    def across_start(turn, column):
        for step in range(1, 4):
            row_copy(turn * 3 + step, column, (s + 2 * step) % 8).start()
        halo_start(4 * turn, column)

    def across_wait(turn, column):
        for step in range(1, 4):
            here = (column + 8 - 2 * step) % 8
            row_copy(turn * 3 + step, here, partner).wait_recv()
            halo_start(4 * turn + step, here)

    def coef_copy(k):
        return remote(
            coef_mine,
            coef_parts.at[(t % 4) * 8 + s],
            coef_send.at[k],
            coef_recv.at[(t % 4) * 8 + s],
            (k, quarter),
        )

    def away(k):
        return jnp.logical_not(jnp.logical_and(loops_back, k == t))

    def coef_start(k, _):
        @pl.when(away(k))
        def _():
            coef_copy(k).start()

        return 0

    def list_copy(step):
        return remote(
            lists.at[s],
            lists.at[s],
            list_send.at[step - 1],
            list_recv.at[step - 1],
            (t, (s + step) % 8),
        )

    row_copy(0, s, partner).start()
    lax.fori_loop(0, t_count, coef_start, 0)
    across_start(0, s)
    for step in range(1, 8):
        list_copy(step).start()

    @pl.when(loops_back)
    def _():
        coef_parts[(t % 4) * 8 + s] = coef_mine[...]

    loads[4].wait()
    for i in range(own):
        rank = jnp.int32(0)
        picks = [t * 32 + s * 4 + (i + 1) % own] * EARLY
        lives = [jnp.int32(0)] * EARLY
        for k in range(slot_count):
            body = near_scalar[i, k]
            inside = jnp.where(body >= t * 32, 1, 0) * jnp.where(body < t * 32 + 32, 1, 0)
            for e in range(EARLY):
                hit = inside * jnp.where(rank == e, 1, 0)
                picks[e] = jnp.where(hit == 1, body, picks[e])
                lives[e] = lives[e] + hit
            rank = rank + inside
        for e in range(EARLY):
            chosen[2 * (i * EARLY + e)] = picks[e] - t * 32
            chosen[2 * (i * EARLY + e) + 1] = lives[e]

    target_stage(nodes, own, lambda c: row_geometry[s * COMPS + c], centre, features)
    total[...] = jnp.zeros_like(total)
    worst[...] = jnp.full_like(worst, -1.0)
    for k in range(own * COMPS):
        slots[k] = jnp.full((8, LANES), FAR_AWAY if k % COMPS < 3 else 0.0, F32)
    moment1[...] = jnp.zeros_like(moment1)
    kernel1[...] = jnp.zeros_like(kernel1)

    across_wait(0, s)
    row_copy(0, partner, partner).wait_recv()
    across_start(1, partner)

    for step in range(1, 8):
        remote(
            lists.at[s],
            lists.at[(s + 8 - step) % 8],
            list_send.at[step - 1],
            list_recv.at[step - 1],
            (t, partner),
        ).wait_recv()
    rows = 8 * own
    listed = lists[...].reshape(rows, 128)
    ids = s * 128 + lax.broadcasted_iota(jnp.int32, (rows, 128), 1)
    hit = ids == t * rows + lax.broadcasted_iota(jnp.int32, (rows, 128), 0)
    for k in range(slot_count):
        hit = jnp.logical_or(hit, ids == listed[:, k : k + 1])
    mask[...] = jnp.where(hit, F32(0.0), F32(1.0))

    def coef_wait(k, _):
        @pl.when(jnp.logical_not(jnp.logical_and(loops_back, k == (t % 4) * 8 + s)))
        def _():
            remote(
                coef_mine, coef_parts.at[k], coef_send.at[k], coef_recv.at[k], (t, partner)
            ).wait_recv()

        return 0

    lax.fori_loop(0, t_count, coef_wait, 0)
    coef = coef_parts[0].astype(F32)
    for k in range(1, t_count):
        coef = coef + coef_parts[k].astype(F32)
    loads[6].wait()

    def fold(i, _):
        kept = coef * mask[pl.ds(i, 1), :]
        product = held[i].astype(F32) * kept[None]
        folded[pl.ds(pl.multiple_of(i * 16, 16), 16), :] = jnp.sum(product, axis=1)
        return 0

    lax.fori_loop(0, rows, fold, 0)
    for q in range(4):
        turned = folded[q * 128 : (q + 1) * 128, :].T
        far_mine[q] = jnp.broadcast_to(jnp.sum(turned, axis=0, keepdims=True), (8, 128))

    def far_copy(step):
        other = (s + step) % 8
        return remote(
            far_mine.at[other // 2],
            far_parts.at[step - 1],
            far_send.at[step - 1],
            far_recv.at[step - 1],
            (t, other),
        )

    for step in range(1, 8):
        far_copy(step).start()

    across_wait(1, partner)

    def store(index, source, target):
        copy = pltpu.make_async_copy(source, target, store_sem.at[index])
        copy.start()
        return copy

    stores = [store(0, row_geometry, row_out)]

    def source(m, spread, moment):
        now = jnp.minimum(m, own * EARLY - 1)
        i = now // EARLY
        e = now % EARLY
        body = chosen[2 * now]
        live = chosen[2 * now + 1]
        base = (body // 4) * COMPS
        raw = [row_geometry[base + c, pl.ds(body % 4, 1), :] for c in range(COMPS)]
        scale = live.astype(F32) * jnp.where(m < own * EARLY, F32(1.0), F32(0.0))
        for c in range(3):
            slots[i * COMPS + c, pl.ds(e, 1), :] = raw[c]
            slots[i * COMPS + 3 + c, pl.ds(e, 1), :] = raw[3 + c] * live.astype(F32)
        source_stage(raw, i, scale, centre, worst, spread, moment)

    def target_of(m):
        return jnp.clip(m, 0, own * EARLY - 1) // EARLY

    near_pairs(
        own * EARLY,
        target_of,
        source,
        features,
        total,
        (kernel0, moment0, spread0),
        (kernel1, moment1, spread1),
    )
    stores.append(store(1, total, total_out))
    stores.append(store(2, worst, worst_out))
    stores.append(store(3, slots, slots_out))

    for step in range(1, 8):
        far_copy(step).wait_recv()
    w = far_mine[s // 2]
    for step in range(1, 8):
        w = w + far_parts[step - 1]
    coupled[...] = jnp.where(s % 2 == 1, pltpu.roll(w, 64, 1), w)

    stores.append(store(4, coupled, coupled_out))

    for side in range(2):
        there = t > 0 if side == 0 else t < t_count - 1
        mine = t < t_count - 1 if side == 0 else t > 0
        columns = [
            ((s if index < 4 else partner) + 8 - 2 * (index % 4)) % 8 for index in range(8)
        ]

        @pl.when(there)
        def _():
            for index, column in enumerate(columns):
                halo_copy(side, index, column).wait_recv()

        @pl.when(mine)
        def _():
            for index, column in enumerate(columns):
                halo_copy(side, index, column).wait_send()

    row_copy(0, s, partner).wait_send()
    for turn, column in ((0, s), (1, partner)):
        for step in range(1, 4):
            row_copy(turn * 3 + step, column, partner).wait_send()
    for step in range(1, 8):
        list_copy(step).wait_send()
        far_copy(step).wait_send()

    def coef_sent(k, _):
        @pl.when(away(k))
        def _():
            coef_copy(k).wait_send()

        return 0

    lax.fori_loop(0, t_count, coef_sent, 0)
    for copy in stores:
        copy.wait()


def velocity_kernel(
    nodes,
    near_in,
    row_in,
    halo_in,
    coupled_in,
    early_in,
    worst_in,
    slots_in,
    basis_in,
    out,
    near,
    row_geometry,
    halo_geometry,
    coupled,
    early,
    early_worst,
    early_slots,
    basis,
    used,
    places,
    centre,
    features,
    spread0,
    spread1,
    moment0,
    moment1,
    kernel0,
    kernel1,
    total,
    slots,
    worst,
    columns,
    load_sem,
):
    loads = [
        pltpu.make_async_copy(source, target, load_sem.at[index])
        for index, (source, target) in enumerate(
            (
                (near_in, near),
                (row_in, row_geometry),
                (halo_in, halo_geometry),
                (worst_in, early_worst),
                (slots_in, early_slots),
                (basis_in, basis),
                (coupled_in, coupled),
                (early_in, early),
            )
        )
    ]
    for load in loads:
        load.start()
    t = lax.axis_index("tgt")
    s = lax.axis_index("src")
    own = out.shape[1]
    per_body = near.shape[1]
    total[...] = jnp.zeros_like(total)
    moment1[...] = jnp.zeros_like(moment1)
    kernel1[...] = jnp.zeros_like(kernel1)
    loads[1].wait()
    target_stage(nodes, own, lambda c: row_geometry[s * COMPS + c], centre, features)

    loads[0].wait()

    def listing(k, carry):
        n, rank, taken = carry
        i = k // per_body
        slot = k % per_body
        rank = jnp.where(slot == 0, 0, rank)
        taken = jnp.where(slot == 0, 0, taken)
        body = near[i, slot] - t * 32
        active = near[i, slot] >= 0
        inside = jnp.logical_and(body >= 0, body < 32)
        early_one = jnp.logical_and(inside, rank < EARLY)
        left = jnp.logical_and(active, jnp.logical_not(early_one))

        @pl.when(left)
        def _():
            used[n] = k
            places[n] = 7 - taken

        more = jnp.where(left, 1, 0)
        return n + more, rank + jnp.where(inside, 1, 0), taken + more

    zero = jnp.int32(0)
    n, _, _ = lax.fori_loop(0, own * per_body, listing, (zero, zero, zero))
    for k in range(2):
        used[n + k] = 0
        places[n + k] = 8

    for load in loads[2:5]:
        load.wait()
    worst[...] = early_worst[...]
    for k in range(own * COMPS):
        slots[k, 0:8] = early_slots[k]

    def rows_of(body):
        inside = jnp.logical_and(body >= 0, body < 32)
        here = jnp.where(inside, body, 0)
        there = jnp.where(inside, 0, jnp.where(body < 0, body + 32, body))
        base = (here // 4) * COMPS
        halo = (there // 4) * COMPS
        place = body % 4
        return [
            jnp.where(
                inside,
                row_geometry[base + c, pl.ds(place, 1), :],
                halo_geometry[halo + c, pl.ds(place, 1), :],
            )
            for c in range(COMPS)
        ]

    def source(m, spread, moment):
        k = used[m]
        i = k // per_body
        raw = rows_of(near[i, k % per_body] - t * 32)
        for c in range(COMPS):
            slots[i * COMPS + c, pl.ds(places[m], 1), :] = raw[c]
        live = jnp.where(m < n, F32(1.0), F32(0.0))
        source_stage(raw, i, live, centre, worst, spread, moment)

    near_pairs(
        n,
        lambda m: used[jnp.maximum(m, 0)] // per_body,
        source,
        features,
        total,
        (kernel0, moment0, spread0),
        (kernel1, moment1, spread1),
    )

    for load in loads[5:]:
        load.wait()
    row8 = lax.broadcasted_iota(jnp.int32, (8, 128), 0)
    lane8 = lax.broadcasted_iota(jnp.int32, (8, 128), 1)
    diagonal = jnp.where(lane8 // 16 == row8, coupled[...], 0.0).astype(BF16)[:, :64]
    far = []
    for c in range(3):
        flat = jnp.concatenate([basis[i, c] for i in range(own)], axis=0)
        far.append(jnp.dot(diagonal, flat, preferred_element_type=F32))

    for i in range(own):
        y = [slots[i * COMPS + c, 0:8] for c in range(3)]
        w = [slots[i * COMPS + 3 + c, 0:8] for c in range(3)]
        sums = [[], [], []]
        for node in range(MAIN, nodes):
            d = [
                row_geometry[s * COMPS + c, i : i + 1, node : node + 1] - y[c] for c in range(3)
            ]
            inverse = lax.rsqrt(d[0] * d[0] + d[1] * d[1] + d[2] * d[2])
            pull = (d[0] * w[0] + d[1] * w[1] + d[2] * w[2]) * (inverse * inverse * inverse)
            for c in range(3):
                value = w[c] * inverse + d[c] * pull
                summed = jnp.sum(value, axis=0, keepdims=True)
                sums[c].append(jnp.sum(summed, axis=1, keepdims=True))
        for c in range(3):
            tail = jnp.concatenate(sums[c], axis=1)
            out[c, i : i + 1, MAIN:nodes] = tail + far[c][i : i + 1, MAIN:nodes]

    crowded = jnp.max(worst[...]) > 0.0

    @pl.when(jnp.logical_not(crowded))
    def _():
        for i in range(own):
            at = total[i] + early[i]
            g = at[0:24] + at[24:48] + at[48:72]
            x = [
                row_geometry[s * COMPS + c, i : i + 1, :MAIN] - centre[c, i : i + 1, :MAIN]
                for c in range(3)
            ]
            plain = [g[k : k + 1] for k in range(3)]
            first = [[g[b + k : b + k + 1] for k in range(3)] for b in (8, 12, 16)]
            along = [g[b + 3 : b + 4] for b in (0, 8, 12, 16)]
            second = [g[20 + k : 21 + k] for k in range(3)]
            square = x[0] * x[0] + x[1] * x[1] + x[2] * x[2]
            inner = x[0] * plain[0] + x[1] * plain[1] + x[2] * plain[2] - along[0]
            for c in range(3):
                u = square * plain[c] + second[c] + along[1 + c] + x[c] * inner
                for k in range(3):
                    u = u - x[k] * (2.0 * first[k][c] + first[c][k])
                out[c, i : i + 1, :MAIN] = u + far[c][i : i + 1, :MAIN]

    @pl.when(crowded)
    def _():
        for i in range(own):
            for c in range(3):
                out[c, i : i + 1, :MAIN] = far[c][i : i + 1, :MAIN]

        def direct(k, _):
            i = k // per_body
            body = near[i, k % per_body]

            @pl.when(body >= 0)
            def _():
                empty = jnp.zeros((2, LANES), F32)
                rows = rows_of(body - t * 32)
                columns[...] = jnp.concatenate(rows + [empty], axis=0).T
                x = [row_geometry[s * COMPS + c, pl.ds(i, 1), :MAIN] for c in range(3)]

                def eight(q, sums):
                    block = columns[pl.ds(pl.multiple_of(q * 8, 8), 8), :]
                    d = [x[c] - block[:, c : c + 1] for c in range(3)]
                    w = [block[:, 3 + c : 4 + c] for c in range(3)]
                    inverse = lax.rsqrt(d[0] * d[0] + d[1] * d[1] + d[2] * d[2])
                    pull = d[0] * w[0] + d[1] * w[1] + d[2] * w[2]
                    pull = pull * (inverse * inverse * inverse)
                    return tuple(sums[c] + (w[c] * inverse + d[c] * pull) for c in range(3))

                start = tuple(jnp.zeros((8, MAIN), F32) for _ in range(3))
                sums = lax.fori_loop(0, ROWS // 8, eight, start)
                for c in range(3):
                    out[c, pl.ds(i, 1), :MAIN] += jnp.sum(sums[c], axis=0, keepdims=True)

            return 0

        lax.fori_loop(0, own * per_body, direct, 0)


def local(positions, weights, density, near_source, couplings, source_basis, target_basis):
    own, _, nodes = positions.shape
    vmem = pl.BlockSpec(memory_space=pltpu.VMEM)
    hbm = pl.BlockSpec(memory_space=pltpu.HBM)
    dma = pltpu.SemaphoreType.DMA
    turned = (1, 0, 2)
    centred = [
        pltpu.VMEM((4, own, LANES), F32),
        pltpu.VMEM((own, 96, MAIN), BF16),
        pltpu.VMEM((96, ROWS), BF16),
        pltpu.VMEM((96, ROWS), BF16),
        pltpu.VMEM((80, ROWS), BF16),
        pltpu.VMEM((80, ROWS), BF16),
        pltpu.VMEM((ROWS, MAIN), BF16),
        pltpu.VMEM((ROWS, MAIN), BF16),
    ]
    row_geometry, halo_geometry, coupled, early, worst, slots = pl.pallas_call(
        functools.partial(exchange_kernel, nodes),
        out_shape=(
            jax.ShapeDtypeStruct((8 * COMPS, own, LANES), F32),
            jax.ShapeDtypeStruct((16 * COMPS, own, LANES), F32),
            jax.ShapeDtypeStruct((8, 128), F32),
            jax.ShapeDtypeStruct((own, 80, MAIN), F32),
            jax.ShapeDtypeStruct((8, LANES), F32),
            jax.ShapeDtypeStruct((own * COMPS, 8, LANES), F32),
        ),
        in_specs=[hbm] * 6,
        out_specs=(hbm,) * 6,
        scratch_shapes=[
            pltpu.VMEM((8 * COMPS, own, LANES), F32),
            pltpu.VMEM((8, 128), F32),
            pltpu.VMEM((own, 80, MAIN), F32),
            pltpu.VMEM((8, LANES), F32),
            pltpu.VMEM((own * COMPS, 8, LANES), F32),
            pltpu.VMEM((3, own, nodes), F32),
            pltpu.VMEM((own, nodes), F32),
            pltpu.VMEM((3, own, nodes), F32),
            pltpu.VMEM((own, 8), jnp.int32),
            pltpu.SMEM((own, 8), jnp.int32),
            pltpu.VMEM((32, 16, 16, 128), BF16),
            pltpu.VMEM((own, 3, 16, nodes), BF16),
            pltpu.VMEM((16, 128), BF16),
            pltpu.VMEM((32, 16, 128), BF16),
            pltpu.VMEM((8, own, 128), jnp.int32),
            pltpu.VMEM((32, 128), F32),
            pltpu.VMEM((512, 128), F32),
            pltpu.VMEM((4, 8, 128), F32),
            pltpu.VMEM((7, 8, 128), F32),
            pltpu.SMEM((2 * own * EARLY,), jnp.int32),
            *centred,
            dma((7,)),
            dma((5,)),
            dma((7,)),
            dma((7,)),
            dma((32,)),
            dma((32,)),
            dma((7,)),
            dma((7,)),
            dma((7,)),
            dma((7,)),
            dma((16,)),
            dma((16,)),
        ],
        compiler_params=pltpu.CompilerParams(
            collective_id=0, has_side_effects=True, vmem_limit_bytes=VMEM_BYTES
        ),
        name="exchange",
    )(
        positions.transpose(turned),
        weights,
        density.transpose(turned),
        near_source,
        couplings.transpose(0, 2, 3, 1),
        source_basis.transpose(0, 2, 1, 3),
    )
    out = pl.pallas_call(
        functools.partial(velocity_kernel, nodes),
        out_shape=jax.ShapeDtypeStruct((3, own, nodes), F32),
        in_specs=[hbm] * 8,
        out_specs=vmem,
        scratch_shapes=[
            pltpu.SMEM((own, 8), jnp.int32),
            pltpu.VMEM((8 * COMPS, own, LANES), F32),
            pltpu.VMEM((16 * COMPS, own, LANES), F32),
            pltpu.VMEM((8, 128), F32),
            pltpu.VMEM((own, 80, MAIN), F32),
            pltpu.VMEM((8, LANES), F32),
            pltpu.VMEM((own * COMPS, 8, LANES), F32),
            pltpu.VMEM((own, 3, 16, nodes), BF16),
            pltpu.SMEM((40,), jnp.int32),
            pltpu.SMEM((40,), jnp.int32),
            *centred,
            pltpu.VMEM((own, 80, MAIN), F32),
            pltpu.VMEM((own * COMPS, 16, LANES), F32),
            pltpu.VMEM((8, LANES), F32),
            pltpu.VMEM((LANES, 8), F32),
            dma((8,)),
        ],
        compiler_params=pltpu.CompilerParams(vmem_limit_bytes=VMEM_BYTES),
        name="velocity",
    )(
        near_source,
        row_geometry,
        halo_geometry,
        coupled,
        early,
        worst,
        slots,
        target_basis.transpose(0, 2, 1, 3),
    )
    return out.transpose(turned)


def solution(mesh):
    placed = (
        P(("tgt", "src"), None, None),
        P(("tgt", "src"), None),
        P(("tgt", "src"), None, None),
        P(("tgt", "src"), None),
        P("tgt", "src", None, None),
        P(("tgt", "src"), None, None, None),
        P(("tgt", "src"), None, None, None),
    )
    return jax.shard_map(
        local, mesh=mesh, in_specs=placed, out_specs=P(("tgt", "src"), None, None), check_vma=False
    )
```

time: 52.5 us -> 47 us (0.90)
  local copies, waits for them, and re-layouts: 5.48 us -> 0 us
    unnamed x14 -> x0, local copies, waits for them, and re-layouts: 5.48 us -> none
    pallas_call x1, Pallas kernels: 29.9 us -> 33.4 us  [local(): pl.pallas_call(functools.partial(exchange_kernel, nodes), out_shape=(jax....]
    pallas_call x1, Pallas kernels: 16.8 us -> 13.4 us  [local(): pl.pallas_call(functools.partial(velocity_kernel, nodes), out_shape=jax.S...]
where the time goes in v2:
time: 47 us; the launch traced here: 46.9 us
  Pallas kernels  46.9 us (100%)
    pallas_call x1, Pallas kernels, local(): pl.pallas_call(functools.partial(exchange_kernel, nodes), out_shape=(jax....  33.4 us
    pallas_call x1, Pallas kernels, local(): pl.pallas_call(functools.partial(velocity_kernel, nodes), out_shape=jax.S...  13.4 us

profile of v2, /device:TPU:64, one launch (start us, length us, event | category | flops | bytes accessed | tf_op | source)
XLA Modules:
  0.0 46.9 jit_solution(9041956038775720752)
XLA Ops:
  0.0 33.4 %exchange.1 = (f32[48,4,768]{2,1,0:T(4,128)}, f32[96,4,768]{2,1,0:T(4,128)}, f32[8,128]{1,0:T(8,128)}, f32[4,80,640]{2,1,0:T(8,128)}, f32[8,768]{1,0:T(8,128)}, /*index=5*/f32[24,8,768]{2,1,0:T(8,128)}) custom-call(f32[3,4,642]{2,1,0:T(4,128)} %bitcast.9, f32[4,642]{1,0:T(4,128)} %weights_in.1, f32[3,4,642]{2,1,0:T(4,128)} %bitcast.10, s32[4,8]{1,0:T(4,128)} %near_in.3, ...), custom_call_target="tpu_custom_call" | custom-call | tf_op jit(solution)/shard_map/exchange/pallas_call | solution.py:747
  33.5 13.4 %velocity.1 = f32[3,4,642]{2,1,0:T(4,128)} custom-call(s32[4,8]{1,0:T(4,128)} %near_in.3, f32[48,4,768]{2,1,0:T(4,128)} %get-tuple-element.11.row_in, f32[96,4,768]{2,1,0:T(4,128)} %get-tuple-element.12.halo_in, f32[8,128]{1,0:T(8,128)} %get-tuple-element.13.coupled_in, f32[4,80,640]{2,1,0:T(8,128)} %get-tuple-element.14.early_in, ...), custom_call_target="tpu_custom_call" | custom-call | tf_op jit(solution)/shard_map/velocity/pallas_call | solution.py:806

commit v3 on v2

--- a/solution.py
+++ b/solution.py
@@ -15,7 +15,10 @@
 FAR_AWAY = 1000.0
 LEAST_GAP = 0.1
 MOST_RATIO = 70.0
-EARLY = 3
+PHASES = (1, 1, 1, 2)
+FACTORS = 32
+MOMENTS = 48
+EARLY = sum(PHASES)
 CUTS = (0, 208, 432, ROWS)
 VMEM_BYTES = 58 * 2**20
 MESH = pl.DeviceIdType.MESH
@@ -37,6 +40,13 @@
     rest = value - high
     middle = rest.astype(BF16).astype(F32)
     return high, middle, rest - middle
+
+
+def by_quad(sub, first, second, third, fourth):
+    quad = sub % 4
+    return jnp.where(
+        quad == 0, first, jnp.where(quad == 1, second, jnp.where(quad == 2, third, fourth))
+    )
 
 
 def target_stage(nodes, own, load, centre, features):
@@ -52,16 +62,18 @@
         radius = radius + offset * offset
     largest = jnp.max(radius, axis=1, keepdims=True)
     centre[3] = jnp.broadcast_to(jnp.sqrt(largest), (own, LANES))
+    sub = lax.broadcasted_iota(jnp.int32, (8, LANES), 0)
     for i in range(own):
-        x = [offset[i : i + 1, :] for offset in offsets]
-        square = radius[i : i + 1, :]
+        x = [jnp.broadcast_to(offset[i : i + 1, :], (8, LANES)) for offset in offsets]
+        square = jnp.broadcast_to(radius[i : i + 1, :], (8, LANES))
+        high, middle, low = split(by_quad(sub, x[0], x[1], x[2], square))
         one = jnp.ones_like(square)
-        zero = jnp.zeros_like(square)
-        parts = split(jnp.concatenate(x + [one, square, zero, zero, zero], axis=0))
-        empty = jnp.zeros((8, LANES), F32)
-        stack = []
-        for part in parts:
-            stack += [part, part, part, empty]
+        stack = [
+            jnp.where(sub % 4 == 3, one, jnp.where(sub < 4, high, middle)),
+            jnp.where(sub < 3, low, jnp.where(sub == 3, one, high)),
+            jnp.where(sub < 4, middle, jnp.where(sub == 7, low, high)),
+            jnp.zeros_like(square),
+        ]
         features[i] = jnp.concatenate(stack, axis=0).astype(BF16)[:, :MAIN]
 
 
@@ -74,32 +86,40 @@
     size = jnp.broadcast_to(centre[3, pl.ds(i, 1), :], (8, LANES))
     ratio = (reach + size) - MOST_RATIO * jnp.maximum(reach - size, LEAST_GAP)
     worst[...] = jnp.maximum(worst[...], ratio)
+    high, middle, low = split(by_quad(sub, -2.0 * y[0], -2.0 * y[1], -2.0 * y[2], square))
+    one = jnp.ones_like(square)
+    stack = [
+        jnp.where(sub == 7, middle, high),
+        jnp.where(sub < 3, high, jnp.where(sub == 3, low, jnp.where(sub == 7, one, middle))),
+        jnp.where(sub % 4 == 3, one, jnp.where(sub < 4, middle, low)),
+        jnp.zeros_like(square),
+    ]
+    spread[...] = jnp.concatenate(stack, axis=0).astype(BF16)[:, :ROWS]
+    w = [live * value for value in w]
     along = y[0] * w[0] + y[1] * w[1] + y[2] * w[2]
-    left = jnp.where(
-        sub == 0,
-        -2.0 * y[0],
-        jnp.where(
-            sub == 1,
-            -2.0 * y[1],
-            jnp.where(
-                sub == 2,
-                -2.0 * y[2],
-                jnp.where(sub == 3, square, jnp.where(sub == 4, F32(1.0), F32(0.0))),
-            ),
-        ),
-    )
-    empty = jnp.zeros((8, LANES), F32)
-    third = jnp.concatenate(list(split(left)) + [empty], axis=0).astype(BF16)[:, :ROWS]
-    spread[...] = jnp.concatenate([third, third, third], axis=0)
-    quad = sub % 4
-    plain = live * jnp.where(
-        quad == 0, w[0], jnp.where(quad == 1, w[1], jnp.where(quad == 2, w[2], along))
-    )
-    once = plain * jnp.where(sub < 4, y[0], y[1])
-    twice = plain * jnp.where(sub < 4, y[2], square)
-    parts = [split(value) for value in (plain, once, twice)]
-    stack = [parts[q][p] for p in range(3) for q in range(3)] + [empty]
+    plain = by_quad(sub, w[0], w[1], w[2], one)
+    last = [w[c] * square + along * y[c] for c in range(3)]
+    front = plain * jnp.where(sub < 4, one, y[0])
+    front = jnp.where(sub == 3, along, jnp.where(sub == 7, last[0], front))
+    back = plain * jnp.where(sub < 4, y[1], y[2])
+    back = jnp.where(sub == 3, last[1], jnp.where(sub == 7, last[2], back))
+    fronts, backs = split(front), split(back)
+    stack = [value for pair in zip(fronts, backs) for value in pair]
     moment[...] = jnp.concatenate(stack, axis=0).astype(BF16)[:, :ROWS]
+
+
+def last_nodes(nodes, i, load, slots):
+    y = [slots[i * COMPS + c, 0:8] for c in range(3)]
+    w = [slots[i * COMPS + 3 + c, 0:8] for c in range(3)]
+    sums = [[], [], []]
+    for node in range(MAIN, nodes):
+        d = [load(c)[i : i + 1, node : node + 1] - y[c] for c in range(3)]
+        inverse = lax.rsqrt(d[0] * d[0] + d[1] * d[1] + d[2] * d[2])
+        pull = (d[0] * w[0] + d[1] * w[1] + d[2] * w[2]) * (inverse * inverse * inverse)
+        for c in range(3):
+            summed = jnp.sum(w[c] * inverse + d[c] * pull, axis=0, keepdims=True)
+            sums[c].append(jnp.sum(summed, axis=1, keepdims=True))
+    return [jnp.concatenate(values, axis=1) for values in sums]
 
 
 def kernel_chunk(features, spread, kernel, low, high):
@@ -125,6 +145,7 @@
         return 0
 
     halves = (count + 1) // 2
+    second[1][...] = jnp.zeros_like(second[1])
     source(0, first[2], first[1])
     lax.fori_loop(0, halves, turn, 0)
     total[target_of(2 * halves - 1)] += moment_chunk(second[0], second[1], 0, ROWS)
@@ -143,11 +164,15 @@
     coupled_out,
     total_out,
     worst_out,
-    slots_out,
+    tails_out,
+    done_out,
+    own_geometry,
+    partner_geometry,
     row_geometry,
     coupled,
     total,
     worst,
+    tails,
     slots,
     positions,
     weights,
@@ -164,6 +189,7 @@
     far_mine,
     far_parts,
     chosen,
+    done,
     centre,
     features,
     spread0,
@@ -243,22 +269,21 @@
         load.wait()
     pad = jnp.zeros((own, LANES - nodes), F32)
     for c in range(3):
-        row_geometry[s * COMPS + c] = jnp.concatenate([positions[c], pad + FAR_AWAY], axis=1)
-        row_geometry[s * COMPS + 3 + c] = jnp.concatenate(
-            [density[c] * weights[...], pad], axis=1
-        )
+        own_geometry[c] = jnp.concatenate([positions[c], pad + FAR_AWAY], axis=1)
+        own_geometry[3 + c] = jnp.concatenate([density[c] * weights[...], pad], axis=1)
     lists[s] = jnp.concatenate([near[...], jnp.full((own, 120), -1, jnp.int32)], axis=1)
 
     loads[5].wait()
-    lane = lax.broadcasted_iota(jnp.int32, (16, 128), 1)
+    sub16 = lax.broadcasted_iota(jnp.int32, (16, 128), 0)
+    lane16 = lax.broadcasted_iota(jnp.int32, (16, 128), 1)
     spread = jnp.zeros((16, 128), F32)
     for j in range(own):
         product = basis[j, 0].astype(F32) * density[0, j : j + 1, :]
         for c in range(1, 3):
             product = product + basis[j, c].astype(F32) * density[c, j : j + 1, :]
         value = jnp.sum(product, axis=1, keepdims=True)
-        spread = jnp.where(lane == (t % 4) * 32 + s * 4 + j, value, spread)
-    coef_mine[...] = spread.astype(BF16)
+        spread = jnp.where(lane16 == sub16 + 16 * j, value, spread)
+    coef_mine[...] = jnp.sum(spread, axis=0, keepdims=True).astype(BF16).astype(F32)
 
     pl.semaphore_wait(
         barrier,
@@ -269,39 +294,48 @@
         + jnp.where(t < t_count - 1, 1, 0),
     )
 
-    def row_copy(index, column, device):
+    def partner_copy():
         return remote(
-            block(column), block(column), row_send.at[index], row_recv.at[index], (t, device)
+            own_geometry, partner_geometry, row_send.at[0], row_recv.at[0], (t, partner)
         )
 
-    def halo_copy(side, index, column):
+    def row_copy(turn, step, source, column, device):
         return remote(
+            source,
             block(column),
+            row_send.at[turn * 3 + step],
+            row_recv.at[turn * 3 + step],
+            (t, device),
+        )
+
+    def halo_copy(side, index, source, column):
+        return remote(
+            source,
             halo_out.at[pl.ds((side * 8 + column) * COMPS, COMPS)],
             halo_send.at[side * 8 + index],
             halo_recv.at[side * 8 + index],
             (t + 1 - 2 * side, s),
         )
 
-    def halo_start(index, column):
+    def halo_start(index, source, column):
         @pl.when(t < t_count - 1)
         def _():
-            halo_copy(0, index, column).start()
+            halo_copy(0, index, source, column).start()
 
         @pl.when(t > 0)
         def _():
-            halo_copy(1, index, column).start()
-
-    def across_start(turn, column):
+            halo_copy(1, index, source, column).start()
+
+    def across_start(turn, source, column):
         for step in range(1, 4):
-            row_copy(turn * 3 + step, column, (s + 2 * step) % 8).start()
-        halo_start(4 * turn, column)
-
-    def across_wait(turn, column):
+            row_copy(turn, step, source, column, (s + 2 * step) % 8).start()
+        halo_start(4 * turn, source, column)
+
+    def across_wait(turn, source, column):
         for step in range(1, 4):
             here = (column + 8 - 2 * step) % 8
-            row_copy(turn * 3 + step, here, partner).wait_recv()
-            halo_start(4 * turn + step, here)
+            row_copy(turn, step, source, here, partner).wait_recv()
+            halo_start(4 * turn + step, block(here), here)
 
     def coef_copy(k):
         return remote(
@@ -331,44 +365,92 @@
             (t, (s + step) % 8),
         )
 
-    row_copy(0, s, partner).start()
-    lax.fori_loop(0, t_count, coef_start, 0)
-    across_start(0, s)
+    partner_copy().start()
     for step in range(1, 8):
         list_copy(step).start()
+    lax.fori_loop(0, t_count, coef_start, 0)
+    across_start(0, own_geometry, s)
 
     @pl.when(loops_back)
     def _():
         coef_parts[(t % 4) * 8 + s] = coef_mine[...]
 
     loads[4].wait()
-    for i in range(own):
-        rank = jnp.int32(0)
-        picks = [t * 32 + s * 4 + (i + 1) % own] * EARLY
-        lives = [jnp.int32(0)] * EARLY
+
+    def choose(i, _):
+        bodies = [near_scalar[i, k] - t * 32 for k in range(slot_count)]
+        free = [jnp.where(body >= 0, 1, 0) * jnp.where(body < 32, 1, 0) for body in bodies]
+        taken = [jnp.int32(0)] * slot_count
+        first = 0
+        for phase, count in enumerate(PHASES):
+            device = (s, partner, partner, None)[phase]
+            other = s * 4 + (i + 1) % own if phase in (0, 3) else partner * 4
+            for e in range(count):
+                pick = jnp.int32(0) + other
+                live = jnp.int32(0)
+                for k in range(slot_count):
+                    hit = free[k] * (1 - live)
+                    if device is not None:
+                        hit = hit * jnp.where(bodies[k] // 4 == device, 1, 0)
+                    pick = jnp.where(hit == 1, bodies[k], pick)
+                    live = live + hit
+                    free[k] = free[k] - hit
+                    taken[k] = taken[k] + hit
+                place = first * own + i * count + e
+                chosen[2 * place] = pick
+                chosen[2 * place + 1] = live
+            first = first + count
         for k in range(slot_count):
-            body = near_scalar[i, k]
-            inside = jnp.where(body >= t * 32, 1, 0) * jnp.where(body < t * 32 + 32, 1, 0)
-            for e in range(EARLY):
-                hit = inside * jnp.where(rank == e, 1, 0)
-                picks[e] = jnp.where(hit == 1, body, picks[e])
-                lives[e] = lives[e] + hit
-            rank = rank + inside
-        for e in range(EARLY):
-            chosen[2 * (i * EARLY + e)] = picks[e] - t * 32
-            chosen[2 * (i * EARLY + e) + 1] = lives[e]
-
-    target_stage(nodes, own, lambda c: row_geometry[s * COMPS + c], centre, features)
+            done[i, k] = taken[k]
+        return 0
+
+    lax.fori_loop(0, own, choose, 0)
+
+    target_stage(nodes, own, lambda c: own_geometry[c], centre, features)
     total[...] = jnp.zeros_like(total)
     worst[...] = jnp.full_like(worst, -1.0)
     for k in range(own * COMPS):
         slots[k] = jnp.full((8, LANES), FAR_AWAY if k % COMPS < 3 else 0.0, F32)
-    moment1[...] = jnp.zeros_like(moment1)
     kernel1[...] = jnp.zeros_like(kernel1)
 
-    across_wait(0, s)
-    row_copy(0, partner, partner).wait_recv()
-    across_start(1, partner)
+    first_set = (kernel0, moment0, spread0)
+    second_set = (kernel1, moment1, spread1)
+
+    def early_pairs(phase, geometry, device):
+        count = PHASES[phase]
+        first = sum(PHASES[:phase])
+        last = own * count - 1
+
+        def source(m, spread, moment):
+            now = jnp.minimum(m, last)
+            i = now // count
+            e = now % count
+            place = first * own + now
+            body = chosen[2 * place]
+            live = chosen[2 * place + 1].astype(F32)
+            base = 0 if device is not None else (body // 4) * COMPS
+            raw = [geometry[base + c, pl.ds(body % 4, 1), :] for c in range(COMPS)]
+            for c in range(3):
+                slots[i * COMPS + c, pl.ds(first + e, 1), :] = raw[c]
+                slots[i * COMPS + 3 + c, pl.ds(first + e, 1), :] = raw[3 + c] * live
+            scale = live * jnp.where(m <= last, F32(1.0), F32(0.0))
+            source_stage(raw, i, scale, centre, worst, spread, moment)
+
+        def target_of(m):
+            return jnp.clip(m, 0, last) // count
+
+        near_pairs(last + 1, target_of, source, features, total, first_set, second_set)
+
+    early_pairs(0, own_geometry, s)
+
+    across_wait(0, own_geometry, s)
+    partner_copy().wait_recv()
+    across_start(1, partner_geometry, partner)
+    for c in range(COMPS):
+        row_geometry[s * COMPS + c] = own_geometry[c]
+        row_geometry[partner * COMPS + c] = partner_geometry[c]
+
+    early_pairs(1, partner_geometry, partner)
 
     for step in range(1, 8):
         remote(
@@ -396,9 +478,18 @@
         return 0
 
     lax.fori_loop(0, t_count, coef_wait, 0)
-    coef = coef_parts[0].astype(F32)
-    for k in range(1, t_count):
-        coef = coef + coef_parts[k].astype(F32)
+    gathered = coef_parts[...].reshape(t_count, 128).astype(BF16)
+    from_row = lax.broadcasted_iota(jnp.int32, (t_count, 128), 0)
+    to_lane = lax.broadcasted_iota(jnp.int32, (t_count, 128), 1)
+    coef = jnp.zeros((16, 128), F32)
+    for j in range(own):
+        chooser = jnp.where(to_lane == own * from_row + j, F32(1.0), F32(0.0)).astype(BF16)
+        coef = coef + lax.dot_general(
+            gathered[:, 16 * j : 16 * j + 16],
+            chooser,
+            (((0,), (0,)), ((), ())),
+            preferred_element_type=F32,
+        )
     loads[6].wait()
 
     def fold(i, _):
@@ -410,7 +501,7 @@
     lax.fori_loop(0, rows, fold, 0)
     for q in range(4):
         turned = folded[q * 128 : (q + 1) * 128, :].T
-        far_mine[q] = jnp.broadcast_to(jnp.sum(turned, axis=0, keepdims=True), (8, 128))
+        far_mine[q] = jnp.sum(turned, axis=0, keepdims=True)
 
     def far_copy(step):
         other = (s + step) % 8
@@ -425,50 +516,31 @@
     for step in range(1, 8):
         far_copy(step).start()
 
-    across_wait(1, partner)
+    early_pairs(2, partner_geometry, partner)
+    across_wait(1, partner_geometry, partner)
 
     def store(index, source, target):
         copy = pltpu.make_async_copy(source, target, store_sem.at[index])
         copy.start()
         return copy
 
-    stores = [store(0, row_geometry, row_out)]
-
-    def source(m, spread, moment):
-        now = jnp.minimum(m, own * EARLY - 1)
-        i = now // EARLY
-        e = now % EARLY
-        body = chosen[2 * now]
-        live = chosen[2 * now + 1]
-        base = (body // 4) * COMPS
-        raw = [row_geometry[base + c, pl.ds(body % 4, 1), :] for c in range(COMPS)]
-        scale = live.astype(F32) * jnp.where(m < own * EARLY, F32(1.0), F32(0.0))
-        for c in range(3):
-            slots[i * COMPS + c, pl.ds(e, 1), :] = raw[c]
-            slots[i * COMPS + 3 + c, pl.ds(e, 1), :] = raw[3 + c] * live.astype(F32)
-        source_stage(raw, i, scale, centre, worst, spread, moment)
-
-    def target_of(m):
-        return jnp.clip(m, 0, own * EARLY - 1) // EARLY
-
-    near_pairs(
-        own * EARLY,
-        target_of,
-        source,
-        features,
-        total,
-        (kernel0, moment0, spread0),
-        (kernel1, moment1, spread1),
-    )
+    stores = [store(0, row_geometry, row_out), store(5, done, done_out)]
+    early_pairs(3, row_geometry, None)
     stores.append(store(1, total, total_out))
     stores.append(store(2, worst, worst_out))
-    stores.append(store(3, slots, slots_out))
+    for i in range(own):
+        sums = last_nodes(nodes, i, lambda c: own_geometry[c], slots)
+        for c in range(3):
+            empty = jnp.zeros((1, 128 + MAIN - nodes), F32)
+            tails[c, i : i + 1, :] = jnp.concatenate([sums[c], empty], axis=1)
+    stores.append(store(3, tails, tails_out))
 
     for step in range(1, 8):
         far_copy(step).wait_recv()
     w = far_mine[s // 2]
     for step in range(1, 8):
         w = w + far_parts[step - 1]
+    w = jnp.broadcast_to(w, (8, 128))
     coupled[...] = jnp.where(s % 2 == 1, pltpu.roll(w, 64, 1), w)
 
     stores.append(store(4, coupled, coupled_out))
@@ -483,17 +555,17 @@
         @pl.when(there)
         def _():
             for index, column in enumerate(columns):
-                halo_copy(side, index, column).wait_recv()
+                halo_copy(side, index, own_geometry, column).wait_recv()
 
         @pl.when(mine)
         def _():
             for index, column in enumerate(columns):
-                halo_copy(side, index, column).wait_send()
-
-    row_copy(0, s, partner).wait_send()
+                halo_copy(side, index, own_geometry, column).wait_send()
+
+    partner_copy().wait_send()
     for turn, column in ((0, s), (1, partner)):
         for step in range(1, 4):
-            row_copy(turn * 3 + step, column, partner).wait_send()
+            row_copy(turn, step, own_geometry, column, partner).wait_send()
     for step in range(1, 8):
         list_copy(step).wait_send()
         far_copy(step).wait_send()
@@ -518,16 +590,18 @@
     coupled_in,
     early_in,
     worst_in,
-    slots_in,
+    tails_in,
+    done_in,
     basis_in,
     out,
     near,
+    done,
     row_geometry,
     halo_geometry,
     coupled,
     early,
     early_worst,
-    early_slots,
+    early_tail,
     basis,
     used,
     places,
@@ -550,10 +624,11 @@
         for index, (source, target) in enumerate(
             (
                 (near_in, near),
+                (done_in, done),
                 (row_in, row_geometry),
                 (halo_in, halo_geometry),
                 (worst_in, early_worst),
-                (slots_in, early_slots),
+                (tails_in, early_tail),
                 (basis_in, basis),
                 (coupled_in, coupled),
                 (early_in, early),
@@ -567,44 +642,38 @@
     own = out.shape[1]
     per_body = near.shape[1]
     total[...] = jnp.zeros_like(total)
-    moment1[...] = jnp.zeros_like(moment1)
     kernel1[...] = jnp.zeros_like(kernel1)
-    loads[1].wait()
+    loads[2].wait()
     target_stage(nodes, own, lambda c: row_geometry[s * COMPS + c], centre, features)
 
-    loads[0].wait()
+    for load in loads[:2]:
+        load.wait()
 
     def listing(k, carry):
-        n, rank, taken = carry
+        n, taken = carry
         i = k // per_body
         slot = k % per_body
-        rank = jnp.where(slot == 0, 0, rank)
         taken = jnp.where(slot == 0, 0, taken)
-        body = near[i, slot] - t * 32
-        active = near[i, slot] >= 0
-        inside = jnp.logical_and(body >= 0, body < 32)
-        early_one = jnp.logical_and(inside, rank < EARLY)
-        left = jnp.logical_and(active, jnp.logical_not(early_one))
+        left = jnp.logical_and(near[i, slot] >= 0, done[i, slot] == 0)
 
         @pl.when(left)
         def _():
             used[n] = k
-            places[n] = 7 - taken
+            places[n] = taken
 
         more = jnp.where(left, 1, 0)
-        return n + more, rank + jnp.where(inside, 1, 0), taken + more
-
-    zero = jnp.int32(0)
-    n, _, _ = lax.fori_loop(0, own * per_body, listing, (zero, zero, zero))
+        return n + more, taken + more
+
+    n, _ = lax.fori_loop(0, own * per_body, listing, (jnp.int32(0), jnp.int32(0)))
     for k in range(2):
         used[n + k] = 0
         places[n + k] = 8
 
-    for load in loads[2:5]:
+    for load in loads[3:6]:
         load.wait()
     worst[...] = early_worst[...]
     for k in range(own * COMPS):
-        slots[k, 0:8] = early_slots[k]
+        slots[k, 0:8] = jnp.full((8, LANES), FAR_AWAY if k % COMPS < 3 else 0.0, F32)
 
     def rows_of(body):
         inside = jnp.logical_and(body >= 0, body < 32)
@@ -626,9 +695,10 @@
         k = used[m]
         i = k // per_body
         raw = rows_of(near[i, k % per_body] - t * 32)
-        for c in range(COMPS):
+        live = jnp.where(m < n, F32(1.0), F32(0.0))
+        for c in range(3):
             slots[i * COMPS + c, pl.ds(places[m], 1), :] = raw[c]
-        live = jnp.where(m < n, F32(1.0), F32(0.0))
+            slots[i * COMPS + 3 + c, pl.ds(places[m], 1), :] = raw[3 + c] * live
         source_stage(raw, i, live, centre, worst, spread, moment)
 
     near_pairs(
@@ -641,7 +711,7 @@
         (kernel1, moment1, spread1),
     )
 
-    for load in loads[5:]:
+    for load in loads[6:]:
         load.wait()
     row8 = lax.broadcasted_iota(jnp.int32, (8, 128), 0)
     lane8 = lax.broadcasted_iota(jnp.int32, (8, 128), 1)
@@ -652,21 +722,9 @@
         far.append(jnp.dot(diagonal, flat, preferred_element_type=F32))
 
     for i in range(own):
-        y = [slots[i * COMPS + c, 0:8] for c in range(3)]
-        w = [slots[i * COMPS + 3 + c, 0:8] for c in range(3)]
-        sums = [[], [], []]
-        for node in range(MAIN, nodes):
-            d = [
-                row_geometry[s * COMPS + c, i : i + 1, node : node + 1] - y[c] for c in range(3)
-            ]
-            inverse = lax.rsqrt(d[0] * d[0] + d[1] * d[1] + d[2] * d[2])
-            pull = (d[0] * w[0] + d[1] * w[1] + d[2] * w[2]) * (inverse * inverse * inverse)
-            for c in range(3):
-                value = w[c] * inverse + d[c] * pull
-                summed = jnp.sum(value, axis=0, keepdims=True)
-                sums[c].append(jnp.sum(summed, axis=1, keepdims=True))
+        sums = last_nodes(nodes, i, lambda c: row_geometry[s * COMPS + c], slots)
         for c in range(3):
-            tail = jnp.concatenate(sums[c], axis=1)
+            tail = sums[c] + early_tail[c, i : i + 1, 0 : nodes - MAIN]
             out[c, i : i + 1, MAIN:nodes] = tail + far[c][i : i + 1, MAIN:nodes]
 
     crowded = jnp.max(worst[...]) > 0.0
@@ -675,19 +733,18 @@
     def _():
         for i in range(own):
             at = total[i] + early[i]
-            g = at[0:24] + at[24:48] + at[48:72]
+            g = at[0:16] + at[16:32] + at[32:48]
             x = [
                 row_geometry[s * COMPS + c, i : i + 1, :MAIN] - centre[c, i : i + 1, :MAIN]
                 for c in range(3)
             ]
             plain = [g[k : k + 1] for k in range(3)]
-            first = [[g[b + k : b + k + 1] for k in range(3)] for b in (8, 12, 16)]
-            along = [g[b + 3 : b + 4] for b in (0, 8, 12, 16)]
-            second = [g[20 + k : 21 + k] for k in range(3)]
+            first = [[g[b + k : b + k + 1] for k in range(3)] for b in (4, 8, 12)]
+            last = [g[k : k + 1] for k in (7, 11, 15)]
             square = x[0] * x[0] + x[1] * x[1] + x[2] * x[2]
-            inner = x[0] * plain[0] + x[1] * plain[1] + x[2] * plain[2] - along[0]
+            inner = x[0] * plain[0] + x[1] * plain[1] + x[2] * plain[2] - g[3:4]
             for c in range(3):
-                u = square * plain[c] + second[c] + along[1 + c] + x[c] * inner
+                u = square * plain[c] + last[c] + x[c] * inner
                 for k in range(3):
                     u = u - x[k] * (2.0 * first[k][c] + first[c][k])
                 out[c, i : i + 1, :MAIN] = u + far[c][i : i + 1, :MAIN]
@@ -736,31 +793,35 @@
     turned = (1, 0, 2)
     centred = [
         pltpu.VMEM((4, own, LANES), F32),
-        pltpu.VMEM((own, 96, MAIN), BF16),
-        pltpu.VMEM((96, ROWS), BF16),
-        pltpu.VMEM((96, ROWS), BF16),
-        pltpu.VMEM((80, ROWS), BF16),
-        pltpu.VMEM((80, ROWS), BF16),
+        pltpu.VMEM((own, FACTORS, MAIN), BF16),
+        pltpu.VMEM((FACTORS, ROWS), BF16),
+        pltpu.VMEM((FACTORS, ROWS), BF16),
+        pltpu.VMEM((MOMENTS, ROWS), BF16),
+        pltpu.VMEM((MOMENTS, ROWS), BF16),
         pltpu.VMEM((ROWS, MAIN), BF16),
         pltpu.VMEM((ROWS, MAIN), BF16),
     ]
-    row_geometry, halo_geometry, coupled, early, worst, slots = pl.pallas_call(
+    moved = pl.pallas_call(
         functools.partial(exchange_kernel, nodes),
         out_shape=(
             jax.ShapeDtypeStruct((8 * COMPS, own, LANES), F32),
             jax.ShapeDtypeStruct((16 * COMPS, own, LANES), F32),
             jax.ShapeDtypeStruct((8, 128), F32),
-            jax.ShapeDtypeStruct((own, 80, MAIN), F32),
+            jax.ShapeDtypeStruct((own, MOMENTS, MAIN), F32),
             jax.ShapeDtypeStruct((8, LANES), F32),
-            jax.ShapeDtypeStruct((own * COMPS, 8, LANES), F32),
+            jax.ShapeDtypeStruct((3, own, 128), F32),
+            jax.ShapeDtypeStruct((own, 8), jnp.int32),
         ),
         in_specs=[hbm] * 6,
-        out_specs=(hbm,) * 6,
+        out_specs=(hbm,) * 7,
         scratch_shapes=[
+            pltpu.VMEM((COMPS, own, LANES), F32),
+            pltpu.VMEM((COMPS, own, LANES), F32),
             pltpu.VMEM((8 * COMPS, own, LANES), F32),
             pltpu.VMEM((8, 128), F32),
-            pltpu.VMEM((own, 80, MAIN), F32),
+            pltpu.VMEM((own, MOMENTS, MAIN), F32),
             pltpu.VMEM((8, LANES), F32),
+            pltpu.VMEM((3, own, 128), F32),
             pltpu.VMEM((own * COMPS, 8, LANES), F32),
             pltpu.VMEM((3, own, nodes), F32),
             pltpu.VMEM((own, nodes), F32),
@@ -769,17 +830,18 @@
             pltpu.SMEM((own, 8), jnp.int32),
             pltpu.VMEM((32, 16, 16, 128), BF16),
             pltpu.VMEM((own, 3, 16, nodes), BF16),
-            pltpu.VMEM((16, 128), BF16),
-            pltpu.VMEM((32, 16, 128), BF16),
+            pltpu.VMEM((1, 128), F32),
+            pltpu.VMEM((32, 1, 128), F32),
             pltpu.VMEM((8, own, 128), jnp.int32),
             pltpu.VMEM((32, 128), F32),
             pltpu.VMEM((512, 128), F32),
-            pltpu.VMEM((4, 8, 128), F32),
-            pltpu.VMEM((7, 8, 128), F32),
+            pltpu.VMEM((4, 1, 128), F32),
+            pltpu.VMEM((7, 1, 128), F32),
             pltpu.SMEM((2 * own * EARLY,), jnp.int32),
+            pltpu.SMEM((own, 8), jnp.int32),
             *centred,
             dma((7,)),
-            dma((5,)),
+            dma((6,)),
             dma((7,)),
             dma((7,)),
             dma((32,)),
@@ -806,36 +868,32 @@
     out = pl.pallas_call(
         functools.partial(velocity_kernel, nodes),
         out_shape=jax.ShapeDtypeStruct((3, own, nodes), F32),
-        in_specs=[hbm] * 8,
+        in_specs=[hbm] * 9,
         out_specs=vmem,
         scratch_shapes=[
+            pltpu.SMEM((own, 8), jnp.int32),
             pltpu.SMEM((own, 8), jnp.int32),
             pltpu.VMEM((8 * COMPS, own, LANES), F32),
             pltpu.VMEM((16 * COMPS, own, LANES), F32),
             pltpu.VMEM((8, 128), F32),
-            pltpu.VMEM((own, 80, MAIN), F32),
+            pltpu.VMEM((own, MOMENTS, MAIN), F32),
             pltpu.VMEM((8, LANES), F32),
-            pltpu.VMEM((own * COMPS, 8, LANES), F32),
+            pltpu.VMEM((3, own, 128), F32),
             pltpu.VMEM((own, 3, 16, nodes), BF16),
             pltpu.SMEM((40,), jnp.int32),
             pltpu.SMEM((40,), jnp.int32),
             *centred,
-            pltpu.VMEM((own, 80, MAIN), F32),
+            pltpu.VMEM((own, MOMENTS, MAIN), F32),
             pltpu.VMEM((own * COMPS, 16, LANES), F32),
             pltpu.VMEM((8, LANES), F32),
             pltpu.VMEM((LANES, 8), F32),
-            dma((8,)),
+            dma((9,)),
         ],
         compiler_params=pltpu.CompilerParams(vmem_limit_bytes=VMEM_BYTES),
         name="velocity",
     )(
         near_source,
-        row_geometry,
-        halo_geometry,
-        coupled,
-        early,
-        worst,
-        slots,
+        *moved,
         target_basis.transpose(0, 2, 1, 3),
     )
     return out.transpose(turned)

time: 47 us -> 39.2 us (0.83)
  the two profiles are of different devices: /device:TPU:64 before, /device:TPU:8 now
where the time goes in v3:
time: 39.2 us; the launch traced here: 39.1 us
  Pallas kernels  39.1 us (100%)
    pallas_call x1, Pallas kernels, local(): pl.pallas_call(functools.partial(exchange_kernel, nodes), out_shape=(jax....  29.1 us
    pallas_call x1, Pallas kernels, local(): pl.pallas_call(functools.partial(velocity_kernel, nodes), out_shape=jax.S...  9.99 us

profile of v3, /device:TPU:8, one launch (start us, length us, event | category | flops | bytes accessed | tf_op | source)
XLA Modules:
  0.0 39.1 jit_solution(5211711589025985765)
XLA Ops:
  0.0 29.1 %exchange.1 = (f32[48,4,768]{2,1,0:T(4,128)}, f32[96,4,768]{2,1,0:T(4,128)}, f32[8,128]{1,0:T(8,128)}, f32[4,48,640]{2,1,0:T(8,128)}, f32[8,768]{1,0:T(8,128)}, /*index=5*/f32[3,4,128]{2,1,0:T(4,128)}, s32[4,8]{1,0:T(4,128)}) custom-call(f32[3,4,642]{2,1,0:T(4,128)} %bitcast.9, f32[4,642]{1,0:T(4,128)} %weights_in.1, f32[3,4,642]{2,1,0:T(4,128)} %bitcast.10, ...), custom_call_target="tpu_custom_call" | custom-call | tf_op jit(solution)/shard_map/exchange/pallas_call | solution.py:804
  29.1 10.0 %velocity.1 = f32[3,4,642]{2,1,0:T(4,128)} custom-call(s32[4,8]{1,0:T(4,128)} %near_in.3, f32[48,4,768]{2,1,0:T(4,128)} %get-tuple-element.12.row_in, f32[96,4,768]{2,1,0:T(4,128)} %get-tuple-element.13.halo_in, f32[8,128]{1,0:T(8,128)} %get-tuple-element.14.coupled_in, f32[4,48,640]{2,1,0:T(8,128)} %get-tuple-element.15.early_in, ...), custom_call_target="tpu_custom_call" | custom-call | tf_op jit(solution)/shard_map/velocity/pallas_call | solution.py:868

commit v4 on v3

--- a/solution.py
+++ b/solution.py
@@ -15,12 +15,12 @@
 FAR_AWAY = 1000.0
 LEAST_GAP = 0.1
 MOST_RATIO = 70.0
-PHASES = (1, 1, 1, 2)
+PHASES = (2, 1, 1, 1)
 FACTORS = 32
 MOMENTS = 48
 EARLY = sum(PHASES)
-CUTS = (0, 208, 432, ROWS)
-VMEM_BYTES = 58 * 2**20
+CUTS = (0, 256, 512, ROWS)
+VMEM_BYTES = 56 * 2**20
 MESH = pl.DeviceIdType.MESH
 
 
@@ -159,20 +159,15 @@
     near_in,
     couplings_in,
     basis_in,
-    row_out,
-    halo_out,
-    coupled_out,
-    total_out,
-    worst_out,
-    tails_out,
-    done_out,
-    own_geometry,
-    partner_geometry,
     row_geometry,
+    halo_geometry,
     coupled,
     total,
     worst,
     tails,
+    done_out,
+    own_geometry,
+    partner_geometry,
     slots,
     positions,
     weights,
@@ -245,14 +240,15 @@
     for step in range(1, 8):
         greet((t, (s + step) % 8))
 
-    def greet_source(k, _):
-        @pl.when(jnp.logical_not(jnp.logical_and(loops_back, k == (t % 4) * 8 + s)))
+    def every(act, mine):
+        for k in range(t_count - 1):
+            act(k + jnp.where(jnp.logical_and(loops_back, mine <= k), 1, 0))
+
+        @pl.when(jnp.logical_not(loops_back))
         def _():
-            greet((4 * s + k // 8, k % 8))
-
-        return 0
-
-    lax.fori_loop(0, t_count, greet_source, 0)
+            act(t_count - 1)
+
+    as_source = (t % 4) * 8 + s
 
     @pl.when(t > 0)
     def _():
@@ -261,6 +257,8 @@
     @pl.when(t < t_count - 1)
     def _():
         greet((t + 1, s))
+
+    every(lambda k: greet((4 * s + k // 8, k % 8)), as_source)
 
     def block(column):
         return row_geometry.at[pl.ds(column * COMPS, COMPS)]
@@ -311,7 +309,7 @@
     def halo_copy(side, index, source, column):
         return remote(
             source,
-            halo_out.at[pl.ds((side * 8 + column) * COMPS, COMPS)],
+            halo_geometry.at[pl.ds((side * 8 + column) * COMPS, COMPS)],
             halo_send.at[side * 8 + index],
             halo_recv.at[side * 8 + index],
             (t + 1 - 2 * side, s),
@@ -346,16 +344,6 @@
             (k, quarter),
         )
 
-    def away(k):
-        return jnp.logical_not(jnp.logical_and(loops_back, k == t))
-
-    def coef_start(k, _):
-        @pl.when(away(k))
-        def _():
-            coef_copy(k).start()
-
-        return 0
-
     def list_copy(step):
         return remote(
             lists.at[s],
@@ -368,7 +356,7 @@
     partner_copy().start()
     for step in range(1, 8):
         list_copy(step).start()
-    lax.fori_loop(0, t_count, coef_start, 0)
+    every(lambda k: coef_copy(k).start(), t)
     across_start(0, own_geometry, s)
 
     @pl.when(loops_back)
@@ -405,6 +393,8 @@
         return 0
 
     lax.fori_loop(0, own, choose, 0)
+    keep_done = pltpu.make_async_copy(done, done_out, store_sem)
+    keep_done.start()
 
     target_stage(nodes, own, lambda c: own_geometry[c], centre, features)
     total[...] = jnp.zeros_like(total)
@@ -468,16 +458,12 @@
         hit = jnp.logical_or(hit, ids == listed[:, k : k + 1])
     mask[...] = jnp.where(hit, F32(0.0), F32(1.0))
 
-    def coef_wait(k, _):
-        @pl.when(jnp.logical_not(jnp.logical_and(loops_back, k == (t % 4) * 8 + s)))
-        def _():
-            remote(
-                coef_mine, coef_parts.at[k], coef_send.at[k], coef_recv.at[k], (t, partner)
-            ).wait_recv()
-
-        return 0
-
-    lax.fori_loop(0, t_count, coef_wait, 0)
+    def coef_arrival(k):
+        return remote(
+            coef_mine, coef_parts.at[k], coef_send.at[k], coef_recv.at[k], (t, partner)
+        )
+
+    every(lambda k: coef_arrival(k).wait_recv(), as_source)
     gathered = coef_parts[...].reshape(t_count, 128).astype(BF16)
     from_row = lax.broadcasted_iota(jnp.int32, (t_count, 128), 0)
     to_lane = lax.broadcasted_iota(jnp.int32, (t_count, 128), 1)
@@ -516,24 +502,21 @@
     for step in range(1, 8):
         far_copy(step).start()
 
+    across_wait(1, partner_geometry, partner)
+    partner_copy().wait_send()
+    for step in range(1, 4):
+        row_copy(0, step, own_geometry, s, partner).wait_send()
+    for step in range(1, 8):
+        list_copy(step).wait_send()
+    every(lambda k: coef_copy(k).wait_send(), t)
     early_pairs(2, partner_geometry, partner)
-    across_wait(1, partner_geometry, partner)
-
-    def store(index, source, target):
-        copy = pltpu.make_async_copy(source, target, store_sem.at[index])
-        copy.start()
-        return copy
-
-    stores = [store(0, row_geometry, row_out), store(5, done, done_out)]
+
     early_pairs(3, row_geometry, None)
-    stores.append(store(1, total, total_out))
-    stores.append(store(2, worst, worst_out))
     for i in range(own):
         sums = last_nodes(nodes, i, lambda c: own_geometry[c], slots)
         for c in range(3):
             empty = jnp.zeros((1, 128 + MAIN - nodes), F32)
             tails[c, i : i + 1, :] = jnp.concatenate([sums[c], empty], axis=1)
-    stores.append(store(3, tails, tails_out))
 
     for step in range(1, 8):
         far_copy(step).wait_recv()
@@ -543,7 +526,6 @@
     w = jnp.broadcast_to(w, (8, 128))
     coupled[...] = jnp.where(s % 2 == 1, pltpu.roll(w, 64, 1), w)
 
-    stores.append(store(4, coupled, coupled_out))
 
     for side in range(2):
         there = t > 0 if side == 0 else t < t_count - 1
@@ -562,46 +544,28 @@
             for index, column in enumerate(columns):
                 halo_copy(side, index, own_geometry, column).wait_send()
 
-    partner_copy().wait_send()
-    for turn, column in ((0, s), (1, partner)):
-        for step in range(1, 4):
-            row_copy(turn, step, own_geometry, column, partner).wait_send()
+    for step in range(1, 4):
+        row_copy(1, step, partner_geometry, partner, partner).wait_send()
     for step in range(1, 8):
-        list_copy(step).wait_send()
         far_copy(step).wait_send()
 
-    def coef_sent(k, _):
-        @pl.when(away(k))
-        def _():
-            coef_copy(k).wait_send()
-
-        return 0
-
-    lax.fori_loop(0, t_count, coef_sent, 0)
-    for copy in stores:
-        copy.wait()
+    keep_done.wait()
 
 
 def velocity_kernel(
     nodes,
     near_in,
-    row_in,
-    halo_in,
-    coupled_in,
-    early_in,
-    worst_in,
-    tails_in,
-    done_in,
-    basis_in,
-    out,
-    near,
-    done,
     row_geometry,
     halo_geometry,
     coupled,
     early,
     early_worst,
     early_tail,
+    done_in,
+    basis_in,
+    out,
+    near,
+    done,
     basis,
     used,
     places,
@@ -625,13 +589,7 @@
             (
                 (near_in, near),
                 (done_in, done),
-                (row_in, row_geometry),
-                (halo_in, halo_geometry),
-                (worst_in, early_worst),
-                (tails_in, early_tail),
                 (basis_in, basis),
-                (coupled_in, coupled),
-                (early_in, early),
             )
         )
     ]
@@ -643,7 +601,6 @@
     per_body = near.shape[1]
     total[...] = jnp.zeros_like(total)
     kernel1[...] = jnp.zeros_like(kernel1)
-    loads[2].wait()
     target_stage(nodes, own, lambda c: row_geometry[s * COMPS + c], centre, features)
 
     for load in loads[:2]:
@@ -669,8 +626,6 @@
         used[n + k] = 0
         places[n + k] = 8
 
-    for load in loads[3:6]:
-        load.wait()
     worst[...] = early_worst[...]
     for k in range(own * COMPS):
         slots[k, 0:8] = jnp.full((8, LANES), FAR_AWAY if k % COMPS < 3 else 0.0, F32)
@@ -711,8 +666,7 @@
         (kernel1, moment1, spread1),
     )
 
-    for load in loads[6:]:
-        load.wait()
+    loads[2].wait()
     row8 = lax.broadcasted_iota(jnp.int32, (8, 128), 0)
     lane8 = lax.broadcasted_iota(jnp.int32, (8, 128), 1)
     diagonal = jnp.where(lane8 // 16 == row8, coupled[...], 0.0).astype(BF16)[:, :64]
@@ -804,24 +758,19 @@
     moved = pl.pallas_call(
         functools.partial(exchange_kernel, nodes),
         out_shape=(
-            jax.ShapeDtypeStruct((8 * COMPS, own, LANES), F32),
-            jax.ShapeDtypeStruct((16 * COMPS, own, LANES), F32),
-            jax.ShapeDtypeStruct((8, 128), F32),
-            jax.ShapeDtypeStruct((own, MOMENTS, MAIN), F32),
-            jax.ShapeDtypeStruct((8, LANES), F32),
-            jax.ShapeDtypeStruct((3, own, 128), F32),
-            jax.ShapeDtypeStruct((own, 8), jnp.int32),
-        ),
-        in_specs=[hbm] * 6,
-        out_specs=(hbm,) * 7,
-        scratch_shapes=[
-            pltpu.VMEM((COMPS, own, LANES), F32),
-            pltpu.VMEM((COMPS, own, LANES), F32),
             pltpu.VMEM((8 * COMPS, own, LANES), F32),
+            pltpu.VMEM((16 * COMPS, own, LANES), F32),
             pltpu.VMEM((8, 128), F32),
             pltpu.VMEM((own, MOMENTS, MAIN), F32),
             pltpu.VMEM((8, LANES), F32),
             pltpu.VMEM((3, own, 128), F32),
+            pltpu.VMEM((own, 8), jnp.int32),
+        ),
+        in_specs=[hbm] * 6,
+        out_specs=(vmem,) * 7,
+        scratch_shapes=[
+            pltpu.VMEM((COMPS, own, LANES), F32),
+            pltpu.VMEM((COMPS, own, LANES), F32),
             pltpu.VMEM((own * COMPS, 8, LANES), F32),
             pltpu.VMEM((3, own, nodes), F32),
             pltpu.VMEM((own, nodes), F32),
@@ -841,7 +790,7 @@
             pltpu.SMEM((own, 8), jnp.int32),
             *centred,
             dma((7,)),
-            dma((6,)),
+            dma,
             dma((7,)),
             dma((7,)),
             dma((32,)),
@@ -868,17 +817,11 @@
     out = pl.pallas_call(
         functools.partial(velocity_kernel, nodes),
         out_shape=jax.ShapeDtypeStruct((3, own, nodes), F32),
-        in_specs=[hbm] * 9,
+        in_specs=[hbm] + [vmem] * 7 + [hbm],
         out_specs=vmem,
         scratch_shapes=[
             pltpu.SMEM((own, 8), jnp.int32),
             pltpu.SMEM((own, 8), jnp.int32),
-            pltpu.VMEM((8 * COMPS, own, LANES), F32),
-            pltpu.VMEM((16 * COMPS, own, LANES), F32),
-            pltpu.VMEM((8, 128), F32),
-            pltpu.VMEM((own, MOMENTS, MAIN), F32),
-            pltpu.VMEM((8, LANES), F32),
-            pltpu.VMEM((3, own, 128), F32),
             pltpu.VMEM((own, 3, 16, nodes), BF16),
             pltpu.SMEM((40,), jnp.int32),
             pltpu.SMEM((40,), jnp.int32),
@@ -887,9 +830,9 @@
             pltpu.VMEM((own * COMPS, 16, LANES), F32),
             pltpu.VMEM((8, LANES), F32),
             pltpu.VMEM((LANES, 8), F32),
-            dma((9,)),
+            dma((3,)),
         ],
-        compiler_params=pltpu.CompilerParams(vmem_limit_bytes=VMEM_BYTES),
+        compiler_params=pltpu.CompilerParams(vmem_limit_bytes=VMEM_BYTES // 2),
         name="velocity",
     )(
         near_source,

time: 39.2 us -> 37.3 us (0.952)
  the two profiles are of different devices: /device:TPU:8 before, /device:TPU:1 now
where the time goes in v4:
time: 37.3 us; the launch traced here: 37.2 us
  Pallas kernels  37.2 us (100%)
    pallas_call x1, Pallas kernels, local(): pl.pallas_call(functools.partial(exchange_kernel, nodes), out_shape=(pltp...  29.4 us
    pallas_call x1, Pallas kernels, local(): pl.pallas_call(functools.partial(velocity_kernel, nodes), out_shape=jax.S...  7.83 us

profile of v4, /device:TPU:1, one launch (start us, length us, event | category | flops | bytes accessed | tf_op | source)
XLA Modules:
  0.0 37.2 jit_solution(650173864388460582)
XLA Ops:
  0.0 0.0 copy-start.1
  0.0 0.0 copy-start
  0.0 29.4 %exchange.1 = (f32[48,4,768]{2,1,0:T(4,128)S(1)}, f32[96,4,768]{2,1,0:T(4,128)S(1)}, f32[8,128]{1,0:T(8,128)S(1)}, f32[4,48,640]{2,1,0:T(8,128)S(1)}, f32[8,768]...) custom-call(f32[3,4,642]{2,1,0:T(4,128)} %bitcast.9, f32[4,642]{1,0:T(4,128)} %weights_in.1, ...), custom_call_target="tpu_custom_call" | custom-call | tf_op jit(solution)/shard_map/exchange/pallas_call | solution.py:758
  29.4 0.0 copy-done.1
  29.4 0.0 copy-done
  29.4 7.8 %velocity.1 = f32[3,4,642]{2,1,0:T(4,128)} custom-call(s32[4,8]{1,0:T(4,128)S(1)} %copy-done.1, f32[48,4,768]{2,1,0:T(4,128)S(1)} %get-tuple-element.12.row_geometry, f32[96,4,768]{2,1,0:T(4,128)S(1)} %get-tuple-element.13.halo_geometry, f32[8,128]{1,0:T(8,128)S(1)} %get-tuple-element.14.coupled, f32[4,48,640]{2,1,0:T(8,128)S(1)} %get-tuple-element.15.early, ...), custom_call_target="tpu_custom_call" | custom-call | tf_op jit(solution)/shard_map/velocity/pallas_call | solution.py:817
Async XLA Ops:
  0.0 29.4 %copy-start.1 = (s32[4,8]{1,0:T(4,128)S(1)}, s32[4,8]{1,0:T(4,128)}, u32[]{:S(2)}) copy-start(s32[4,8]{1,0:T(4,128)} %near_in.3) | copy-start | bytes 388
  0.0 29.4 %copy-start = (bf16[4,16,3,642]{3,1,2,0:T(8,128)(2,1)S(1)}, bf16[4,16,3,642]{3,1,2,0:T(8,128)(2,1)}, u32[]{:S(2)}) copy-start(bf16[4,16,3,642]{3,1,2,0:T(8,128)(2,1)} %param.13) | copy-start | bytes 739588

commit v5 on v4

--- a/solution.py
+++ b/solution.py
@@ -12,6 +12,8 @@
 ROWS = 656
 MAIN = 640
 COMPS = 6
+TILES = MAIN // 128
+BLOCK = COMPS * TILES + 1
 FAR_AWAY = 1000.0
 LEAST_GAP = 0.1
 MOST_RATIO = 70.0
@@ -35,6 +37,24 @@
     )
 
 
+def turn_lanes(value, shift):
+    rows = value.shape[0]
+    filled = jnp.concatenate([value, jnp.zeros((8 - rows, 128), F32)], axis=0)
+    return pltpu.roll(filled, shift % 128, 1)[:rows]
+
+
+def body_rows(nodes, tile):
+    last = tile(COMPS * TILES)
+    lane = lax.broadcasted_iota(jnp.int32, last.shape, 1)
+    width = nodes - MAIN
+    rows = []
+    for c in range(COMPS):
+        tail = turn_lanes(last, -width * c) if c else last
+        tail = jnp.where(lane < width, tail, FAR_AWAY if c < 3 else 0.0)
+        rows.append(jnp.concatenate([tile(c * TILES + k) for k in range(TILES)] + [tail], axis=1))
+    return rows
+
+
 def split(value):
     high = value.astype(BF16).astype(F32)
     rest = value - high
@@ -49,12 +69,12 @@
     )
 
 
-def target_stage(nodes, own, load, centre, features):
+def target_stage(nodes, own, bodies, centre, features):
     inside = lax.broadcasted_iota(jnp.int32, (own, LANES), 1) < nodes
     radius = jnp.zeros((own, LANES), F32)
     offsets = []
     for c in range(3):
-        value = load(c)
+        value = bodies[c]
         mean = jnp.sum(jnp.where(inside, value, 0.0), axis=1, keepdims=True) / nodes
         centre[c] = jnp.broadcast_to(mean, (own, LANES))
         offset = jnp.where(inside, value - mean, 0.0)
@@ -108,12 +128,12 @@
     moment[...] = jnp.concatenate(stack, axis=0).astype(BF16)[:, :ROWS]
 
 
-def last_nodes(nodes, i, load, slots):
+def last_nodes(nodes, i, bodies, slots):
     y = [slots[i * COMPS + c, 0:8] for c in range(3)]
     w = [slots[i * COMPS + 3 + c, 0:8] for c in range(3)]
     sums = [[], [], []]
     for node in range(MAIN, nodes):
-        d = [load(c)[i : i + 1, node : node + 1] - y[c] for c in range(3)]
+        d = [bodies[c][i : i + 1, node : node + 1] - y[c] for c in range(3)]
         inverse = lax.rsqrt(d[0] * d[0] + d[1] * d[1] + d[2] * d[2])
         pull = (d[0] * w[0] + d[1] * w[1] + d[2] * w[2]) * (inverse * inverse * inverse)
         for c in range(3):
@@ -261,14 +281,19 @@
     every(lambda k: greet((4 * s + k // 8, k % 8)), as_source)
 
     def block(column):
-        return row_geometry.at[pl.ds(column * COMPS, COMPS)]
+        return row_geometry.at[pl.ds(column * BLOCK, BLOCK)]
 
     for load in loads[:4]:
         load.wait()
     pad = jnp.zeros((own, LANES - nodes), F32)
-    for c in range(3):
-        own_geometry[c] = jnp.concatenate([positions[c], pad + FAR_AWAY], axis=1)
-        own_geometry[3 + c] = jnp.concatenate([density[c] * weights[...], pad], axis=1)
+    tails_mine = jnp.zeros((own, 128), F32)
+    for c in range(COMPS):
+        value = positions[c] if c < 3 else density[c - 3] * weights[...]
+        value = jnp.concatenate([value, pad], axis=1)
+        for k in range(TILES):
+            own_geometry[c * TILES + k] = value[:, 128 * k : 128 * k + 128]
+        tails_mine = tails_mine + turn_lanes(value[:, MAIN:], (nodes - MAIN) * c)
+    own_geometry[COMPS * TILES] = tails_mine
     lists[s] = jnp.concatenate([near[...], jnp.full((own, 120), -1, jnp.int32)], axis=1)
 
     loads[5].wait()
@@ -282,86 +307,6 @@
         value = jnp.sum(product, axis=1, keepdims=True)
         spread = jnp.where(lane16 == sub16 + 16 * j, value, spread)
     coef_mine[...] = jnp.sum(spread, axis=0, keepdims=True).astype(BF16).astype(F32)
-
-    pl.semaphore_wait(
-        barrier,
-        7
-        + t_count
-        - jnp.where(loops_back, 1, 0)
-        + jnp.where(t > 0, 1, 0)
-        + jnp.where(t < t_count - 1, 1, 0),
-    )
-
-    def partner_copy():
-        return remote(
-            own_geometry, partner_geometry, row_send.at[0], row_recv.at[0], (t, partner)
-        )
-
-    def row_copy(turn, step, source, column, device):
-        return remote(
-            source,
-            block(column),
-            row_send.at[turn * 3 + step],
-            row_recv.at[turn * 3 + step],
-            (t, device),
-        )
-
-    def halo_copy(side, index, source, column):
-        return remote(
-            source,
-            halo_geometry.at[pl.ds((side * 8 + column) * COMPS, COMPS)],
-            halo_send.at[side * 8 + index],
-            halo_recv.at[side * 8 + index],
-            (t + 1 - 2 * side, s),
-        )
-
-    def halo_start(index, source, column):
-        @pl.when(t < t_count - 1)
-        def _():
-            halo_copy(0, index, source, column).start()
-
-        @pl.when(t > 0)
-        def _():
-            halo_copy(1, index, source, column).start()
-
-    def across_start(turn, source, column):
-        for step in range(1, 4):
-            row_copy(turn, step, source, column, (s + 2 * step) % 8).start()
-        halo_start(4 * turn, source, column)
-
-    def across_wait(turn, source, column):
-        for step in range(1, 4):
-            here = (column + 8 - 2 * step) % 8
-            row_copy(turn, step, source, here, partner).wait_recv()
-            halo_start(4 * turn + step, block(here), here)
-
-    def coef_copy(k):
-        return remote(
-            coef_mine,
-            coef_parts.at[(t % 4) * 8 + s],
-            coef_send.at[k],
-            coef_recv.at[(t % 4) * 8 + s],
-            (k, quarter),
-        )
-
-    def list_copy(step):
-        return remote(
-            lists.at[s],
-            lists.at[s],
-            list_send.at[step - 1],
-            list_recv.at[step - 1],
-            (t, (s + step) % 8),
-        )
-
-    partner_copy().start()
-    for step in range(1, 8):
-        list_copy(step).start()
-    every(lambda k: coef_copy(k).start(), t)
-    across_start(0, own_geometry, s)
-
-    @pl.when(loops_back)
-    def _():
-        coef_parts[(t % 4) * 8 + s] = coef_mine[...]
 
     loads[4].wait()
 
@@ -396,12 +341,93 @@
     keep_done = pltpu.make_async_copy(done, done_out, store_sem)
     keep_done.start()
 
-    target_stage(nodes, own, lambda c: own_geometry[c], centre, features)
+    bodies = body_rows(nodes, lambda k: own_geometry[k])
+    target_stage(nodes, own, bodies, centre, features)
     total[...] = jnp.zeros_like(total)
     worst[...] = jnp.full_like(worst, -1.0)
     for k in range(own * COMPS):
         slots[k] = jnp.full((8, LANES), FAR_AWAY if k % COMPS < 3 else 0.0, F32)
     kernel1[...] = jnp.zeros_like(kernel1)
+
+    pl.semaphore_wait(
+        barrier,
+        7
+        + t_count
+        - jnp.where(loops_back, 1, 0)
+        + jnp.where(t > 0, 1, 0)
+        + jnp.where(t < t_count - 1, 1, 0),
+    )
+
+    def partner_copy():
+        return remote(
+            own_geometry, partner_geometry, row_send.at[0], row_recv.at[0], (t, partner)
+        )
+
+    def row_copy(turn, step, source, column, device):
+        return remote(
+            source,
+            block(column),
+            row_send.at[turn * 3 + step],
+            row_recv.at[turn * 3 + step],
+            (t, device),
+        )
+
+    def halo_copy(side, index, source, column):
+        return remote(
+            source,
+            halo_geometry.at[pl.ds((side * 8 + column) * BLOCK, BLOCK)],
+            halo_send.at[side * 8 + index],
+            halo_recv.at[side * 8 + index],
+            (t + 1 - 2 * side, s),
+        )
+
+    def halo_start(index, source, column):
+        @pl.when(t < t_count - 1)
+        def _():
+            halo_copy(0, index, source, column).start()
+
+        @pl.when(t > 0)
+        def _():
+            halo_copy(1, index, source, column).start()
+
+    def across_start(turn, source, column):
+        for step in range(1, 4):
+            row_copy(turn, step, source, column, (s + 2 * step) % 8).start()
+        halo_start(4 * turn, source, column)
+
+    def across_wait(turn, source, column):
+        for step in range(1, 4):
+            here = (column + 8 - 2 * step) % 8
+            row_copy(turn, step, source, here, partner).wait_recv()
+            halo_start(4 * turn + step, block(here), here)
+
+    def coef_copy(k):
+        return remote(
+            coef_mine,
+            coef_parts.at[(t % 4) * 8 + s],
+            coef_send.at[k],
+            coef_recv.at[(t % 4) * 8 + s],
+            (k, quarter),
+        )
+
+    def list_copy(step):
+        return remote(
+            lists.at[s],
+            lists.at[s],
+            list_send.at[step - 1],
+            list_recv.at[step - 1],
+            (t, (s + step) % 8),
+        )
+
+    partner_copy().start()
+    every(lambda k: coef_copy(k).start(), t)
+    across_start(0, own_geometry, s)
+    for step in range(1, 8):
+        list_copy(step).start()
+
+    @pl.when(loops_back)
+    def _():
+        coef_parts[(t % 4) * 8 + s] = coef_mine[...]
 
     first_set = (kernel0, moment0, spread0)
     second_set = (kernel1, moment1, spread1)
@@ -418,8 +444,8 @@
             place = first * own + now
             body = chosen[2 * place]
             live = chosen[2 * place + 1].astype(F32)
-            base = 0 if device is not None else (body // 4) * COMPS
-            raw = [geometry[base + c, pl.ds(body % 4, 1), :] for c in range(COMPS)]
+            base = 0 if device is not None else (body // 4) * BLOCK
+            raw = body_rows(nodes, lambda k: geometry[base + k, pl.ds(body % 4, 1), :])
             for c in range(3):
                 slots[i * COMPS + c, pl.ds(first + e, 1), :] = raw[c]
                 slots[i * COMPS + 3 + c, pl.ds(first + e, 1), :] = raw[3 + c] * live
@@ -436,9 +462,9 @@
     across_wait(0, own_geometry, s)
     partner_copy().wait_recv()
     across_start(1, partner_geometry, partner)
-    for c in range(COMPS):
-        row_geometry[s * COMPS + c] = own_geometry[c]
-        row_geometry[partner * COMPS + c] = partner_geometry[c]
+    for k in range(BLOCK):
+        row_geometry[s * BLOCK + k] = own_geometry[k]
+        row_geometry[partner * BLOCK + k] = partner_geometry[k]
 
     early_pairs(1, partner_geometry, partner)
 
@@ -513,7 +539,7 @@
 
     early_pairs(3, row_geometry, None)
     for i in range(own):
-        sums = last_nodes(nodes, i, lambda c: own_geometry[c], slots)
+        sums = last_nodes(nodes, i, bodies, slots)
         for c in range(3):
             empty = jnp.zeros((1, 128 + MAIN - nodes), F32)
             tails[c, i : i + 1, :] = jnp.concatenate([sums[c], empty], axis=1)
@@ -601,7 +627,8 @@
     per_body = near.shape[1]
     total[...] = jnp.zeros_like(total)
     kernel1[...] = jnp.zeros_like(kernel1)
-    target_stage(nodes, own, lambda c: row_geometry[s * COMPS + c], centre, features)
+    bodies = body_rows(nodes, lambda k: row_geometry[s * BLOCK + k])
+    target_stage(nodes, own, bodies, centre, features)
 
     for load in loads[:2]:
         load.wait()
@@ -613,11 +640,8 @@
         taken = jnp.where(slot == 0, 0, taken)
         left = jnp.logical_and(near[i, slot] >= 0, done[i, slot] == 0)
 
-        @pl.when(left)
-        def _():
-            used[n] = k
-            places[n] = taken
-
+        used[n] = k
+        places[n] = taken
         more = jnp.where(left, 1, 0)
         return n + more, taken + more
 
@@ -634,17 +658,17 @@
         inside = jnp.logical_and(body >= 0, body < 32)
         here = jnp.where(inside, body, 0)
         there = jnp.where(inside, 0, jnp.where(body < 0, body + 32, body))
-        base = (here // 4) * COMPS
-        halo = (there // 4) * COMPS
+        base = (here // 4) * BLOCK
+        halo = (there // 4) * BLOCK
         place = body % 4
-        return [
-            jnp.where(
+        return body_rows(
+            nodes,
+            lambda k: jnp.where(
                 inside,
-                row_geometry[base + c, pl.ds(place, 1), :],
-                halo_geometry[halo + c, pl.ds(place, 1), :],
-            )
-            for c in range(COMPS)
-        ]
+                row_geometry[base + k, pl.ds(place, 1), :],
+                halo_geometry[halo + k, pl.ds(place, 1), :],
+            ),
+        )
 
     def source(m, spread, moment):
         k = used[m]
@@ -676,7 +700,7 @@
         far.append(jnp.dot(diagonal, flat, preferred_element_type=F32))
 
     for i in range(own):
-        sums = last_nodes(nodes, i, lambda c: row_geometry[s * COMPS + c], slots)
+        sums = last_nodes(nodes, i, bodies, slots)
         for c in range(3):
             tail = sums[c] + early_tail[c, i : i + 1, 0 : nodes - MAIN]
             out[c, i : i + 1, MAIN:nodes] = tail + far[c][i : i + 1, MAIN:nodes]
@@ -689,8 +713,7 @@
             at = total[i] + early[i]
             g = at[0:16] + at[16:32] + at[32:48]
             x = [
-                row_geometry[s * COMPS + c, i : i + 1, :MAIN] - centre[c, i : i + 1, :MAIN]
-                for c in range(3)
+                bodies[c][i : i + 1, :MAIN] - centre[c, i : i + 1, :MAIN] for c in range(3)
             ]
             plain = [g[k : k + 1] for k in range(3)]
             first = [[g[b + k : b + k + 1] for k in range(3)] for b in (4, 8, 12)]
@@ -718,7 +741,16 @@
                 empty = jnp.zeros((2, LANES), F32)
                 rows = rows_of(body - t * 32)
                 columns[...] = jnp.concatenate(rows + [empty], axis=0).T
-                x = [row_geometry[s * COMPS + c, pl.ds(i, 1), :MAIN] for c in range(3)]
+                x = [
+                    jnp.concatenate(
+                        [
+                            row_geometry[s * BLOCK + c * TILES + k, pl.ds(i, 1), :]
+                            for k in range(TILES)
+                        ],
+                        axis=1,
+                    )
+                    for c in range(3)
+                ]
 
                 def eight(q, sums):
                     block = columns[pl.ds(pl.multiple_of(q * 8, 8), 8), :]
@@ -758,8 +790,8 @@
     moved = pl.pallas_call(
         functools.partial(exchange_kernel, nodes),
         out_shape=(
-            pltpu.VMEM((8 * COMPS, own, LANES), F32),
-            pltpu.VMEM((16 * COMPS, own, LANES), F32),
+            pltpu.VMEM((8 * BLOCK, own, 128), F32),
+            pltpu.VMEM((16 * BLOCK, own, 128), F32),
             pltpu.VMEM((8, 128), F32),
             pltpu.VMEM((own, MOMENTS, MAIN), F32),
             pltpu.VMEM((8, LANES), F32),
@@ -769,8 +801,8 @@
         in_specs=[hbm] * 6,
         out_specs=(vmem,) * 7,
         scratch_shapes=[
-            pltpu.VMEM((COMPS, own, LANES), F32),
-            pltpu.VMEM((COMPS, own, LANES), F32),
+            pltpu.VMEM((BLOCK, own, 128), F32),
+            pltpu.VMEM((BLOCK, own, 128), F32),
             pltpu.VMEM((own * COMPS, 8, LANES), F32),
             pltpu.VMEM((3, own, nodes), F32),
             pltpu.VMEM((own, nodes), F32),

time: 37.3 us -> 36.7 us (0.984)
  the two profiles are of different devices: /device:TPU:1 before, /device:TPU:64 now
where the time goes in v5:
time: 36.7 us; the launch traced here: 36.1 us
  Pallas kernels  36 us (98%)
    pallas_call x1, Pallas kernels, local(): pl.pallas_call(functools.partial(exchange_kernel, nodes), out_shape=(pltp...  28.1 us
    pallas_call x1, Pallas kernels, local(): pl.pallas_call(functools.partial(velocity_kernel, nodes), out_shape=jax.S...  7.99 us

profile of v5, /device:TPU:64, one launch (start us, length us, event | category | flops | bytes accessed | tf_op | source)
XLA Modules:
  0.0 36.1 jit_solution(6285629882379900380)
XLA Ops:
  0.0 0.0 copy-start.1
  0.0 0.0 copy-start
  0.0 28.1 %exchange.1 = (f32[248,4,128]{2,1,0:T(4,128)S(1)}, f32[496,4,128]{2,1,0:T(4,128)S(1)}, f32[8,128]{1,0:T(8,128)S(1)}, f32[4,48,640]{2,1,0:T(8,128)S(1)}, f32[8,76...) custom-call(f32[3,4,642]{2,1,0:T(4,128)} %bitcast.9, f32[4,642]{1,0:T(4,128)} %weights_in.1, ...), custom_call_target="tpu_custom_call" | custom-call | tf_op jit(solution)/shard_map/exchange/pallas_call | solution.py:790
  28.1 0.0 copy-done.1
  28.1 0.0 copy-done
  28.1 8.0 %velocity.1 = f32[3,4,642]{2,1,0:T(4,128)} custom-call(s32[4,8]{1,0:T(4,128)S(1)} %copy-done.1, f32[248,4,128]{2,1,0:T(4,128)S(1)} %get-tuple-element.12.row_geometry, f32[496,4,128]{2,1,0:T(4,128)S(1)} %get-tuple-element.13.halo_geometry, f32[8,128]{1,0:T(8,128)S(1)} %get-tuple-element.14.coupled, f32[4,48,640]{2,1,0:T(8,128)S(1)} %get-tuple-element.15.early, ...), custom_call_target="tpu_custom_call" | custom-call | tf_op jit(solution)/shard_map/velocity/pallas_call | solution.py:849
Async XLA Ops:
  0.0 28.1 %copy-start.1 = (s32[4,8]{1,0:T(4,128)S(1)}, s32[4,8]{1,0:T(4,128)}, u32[]{:S(2)}) copy-start(s32[4,8]{1,0:T(4,128)} %near_in.3) | copy-start | bytes 388
  0.0 28.1 %copy-start = (bf16[4,16,3,642]{3,1,2,0:T(8,128)(2,1)S(1)}, bf16[4,16,3,642]{3,1,2,0:T(8,128)(2,1)}, u32[]{:S(2)}) copy-start(bf16[4,16,3,642]{3,1,2,0:T(8,128)(2,1)} %param.13) | copy-start | bytes 739588

commit v6 on v5

--- a/solution.py
+++ b/solution.py
@@ -186,6 +186,8 @@
     worst,
     tails,
     done_out,
+    centre,
+    features,
     own_geometry,
     partner_geometry,
     slots,
@@ -205,8 +207,6 @@
     far_parts,
     chosen,
     done,
-    centre,
-    features,
     spread0,
     spread1,
     moment0,
@@ -588,6 +588,8 @@
     early_worst,
     early_tail,
     done_in,
+    centre,
+    features,
     basis_in,
     out,
     near,
@@ -595,8 +597,6 @@
     basis,
     used,
     places,
-    centre,
-    features,
     spread0,
     spread1,
     moment0,
@@ -628,24 +628,20 @@
     total[...] = jnp.zeros_like(total)
     kernel1[...] = jnp.zeros_like(kernel1)
     bodies = body_rows(nodes, lambda k: row_geometry[s * BLOCK + k])
-    target_stage(nodes, own, bodies, centre, features)
 
     for load in loads[:2]:
         load.wait()
 
-    def listing(k, carry):
-        n, taken = carry
-        i = k // per_body
-        slot = k % per_body
-        taken = jnp.where(slot == 0, 0, taken)
-        left = jnp.logical_and(near[i, slot] >= 0, done[i, slot] == 0)
-
-        used[n] = k
-        places[n] = taken
-        more = jnp.where(left, 1, 0)
-        return n + more, taken + more
-
-    n, _ = lax.fori_loop(0, own * per_body, listing, (jnp.int32(0), jnp.int32(0)))
+    n = jnp.int32(0)
+    for i in range(own):
+        taken = jnp.int32(0)
+        for slot in range(per_body):
+            left = jnp.logical_and(near[i, slot] >= 0, done[i, slot] == 0)
+            used[n] = i * per_body + slot
+            places[n] = taken
+            more = jnp.where(left, 1, 0)
+            n = n + more
+            taken = taken + more
     for k in range(2):
         used[n + k] = 0
         places[n + k] = 8
@@ -777,9 +773,7 @@
     hbm = pl.BlockSpec(memory_space=pltpu.HBM)
     dma = pltpu.SemaphoreType.DMA
     turned = (1, 0, 2)
-    centred = [
-        pltpu.VMEM((4, own, LANES), F32),
-        pltpu.VMEM((own, FACTORS, MAIN), BF16),
+    pair_buffers = [
         pltpu.VMEM((FACTORS, ROWS), BF16),
         pltpu.VMEM((FACTORS, ROWS), BF16),
         pltpu.VMEM((MOMENTS, ROWS), BF16),
@@ -797,9 +791,11 @@
             pltpu.VMEM((8, LANES), F32),
             pltpu.VMEM((3, own, 128), F32),
             pltpu.VMEM((own, 8), jnp.int32),
+            pltpu.VMEM((4, own, LANES), F32),
+            pltpu.VMEM((own, FACTORS, MAIN), BF16),
         ),
         in_specs=[hbm] * 6,
-        out_specs=(vmem,) * 7,
+        out_specs=(vmem,) * 9,
         scratch_shapes=[
             pltpu.VMEM((BLOCK, own, 128), F32),
             pltpu.VMEM((BLOCK, own, 128), F32),
@@ -820,7 +816,7 @@
             pltpu.VMEM((7, 1, 128), F32),
             pltpu.SMEM((2 * own * EARLY,), jnp.int32),
             pltpu.SMEM((own, 8), jnp.int32),
-            *centred,
+            *pair_buffers,
             dma((7,)),
             dma,
             dma((7,)),
@@ -849,7 +845,7 @@
     out = pl.pallas_call(
         functools.partial(velocity_kernel, nodes),
         out_shape=jax.ShapeDtypeStruct((3, own, nodes), F32),
-        in_specs=[hbm] + [vmem] * 7 + [hbm],
+        in_specs=[hbm] + [vmem] * 9 + [hbm],
         out_specs=vmem,
         scratch_shapes=[
             pltpu.SMEM((own, 8), jnp.int32),
@@ -857,7 +853,7 @@
             pltpu.VMEM((own, 3, 16, nodes), BF16),
             pltpu.SMEM((40,), jnp.int32),
             pltpu.SMEM((40,), jnp.int32),
-            *centred,
+            *pair_buffers,
             pltpu.VMEM((own, MOMENTS, MAIN), F32),
             pltpu.VMEM((own * COMPS, 16, LANES), F32),
             pltpu.VMEM((8, LANES), F32),

time: 36.7 us -> 36.6 us (level)
  the two profiles are of different devices: /device:TPU:64 before, /device:TPU:1 now
where the time goes in v6:
time: 36.6 us; the launch traced here: 36.5 us
  Pallas kernels  36.4 us (99%)
    pallas_call x1, Pallas kernels, local(): pl.pallas_call(functools.partial(exchange_kernel, nodes), out_shape=(pltp...  28.8 us
    pallas_call x1, Pallas kernels, local(): pl.pallas_call(functools.partial(velocity_kernel, nodes), out_shape=jax.S...  7.61 us

profile of v6, /device:TPU:1, one launch (start us, length us, event | category | flops | bytes accessed | tf_op | source)
XLA Modules:
  0.0 36.5 jit_solution(11603589741343529824)
XLA Ops:
  0.0 0.0 copy-start.1
  0.0 0.0 copy-start
  0.0 28.8 %exchange.1 = (f32[248,4,128]{2,1,0:T(4,128)S(1)}, f32[496,4,128]{2,1,0:T(4,128)S(1)}, f32[8,128]{1,0:T(8,128)S(1)}, f32[4,48,640]{2,1,0:T(8,128)S(1)}, f32[8,76...) custom-call(f32[3,4,642]{2,1,0:T(4,128)} %bitcast.9, ...), custom_call_target="tpu_custom_call" | custom-call | tf_op jit(solution)/shard_map/exchange/pallas_call | solution.py:784
  28.8 0.0 copy-done.1
  28.8 0.0 copy-done
  28.8 7.6 %velocity.1 = f32[3,4,642]{2,1,0:T(4,128)} custom-call(s32[4,8]{1,0:T(4,128)S(1)} %copy-done.1, f32[248,4,128]{2,1,0:T(4,128)S(1)} %get-tuple-element.14.row_geometry, f32[496,4,128]{2,1,0:T(4,128)S(1)} %get-tuple-element.15.halo_geometry, f32[8,128]{1,0:T(8,128)S(1)} %get-tuple-element.16.coupled, f32[4,48,640]{2,1,0:T(8,128)S(1)} %get-tuple-element.17.early, ...), custom_call_target="tpu_custom_call" | custom-call | tf_op jit(solution)/shard_map/velocity/pallas_call | solution.py:845
Async XLA Ops:
  0.0 28.8 %copy-start.1 = (s32[4,8]{1,0:T(4,128)S(1)}, s32[4,8]{1,0:T(4,128)}, u32[]{:S(2)}) copy-start(s32[4,8]{1,0:T(4,128)} %near_in.3) | copy-start | bytes 388
  0.0 28.8 %copy-start = (bf16[4,16,3,642]{3,1,2,0:T(8,128)(2,1)S(1)}, bf16[4,16,3,642]{3,1,2,0:T(8,128)(2,1)}, u32[]{:S(2)}) copy-start(bf16[4,16,3,642]{3,1,2,0:T(8,128)(2,1)} %param.13) | copy-start | bytes 739588
